TPU v7x, 256 devices: a whole 4x4x8 slice. The times are simulated.
256 devices in a mesh: row: 8 (over y, core), col: 32 (over x, z).
Axes of the slice: x: 4, y: 4, z: 8, core: 2. Of those that a mesh axis runs over, the one named last changes fastest.
Arguments:
- covariance: float32 [16384, 16384], P('row', 'col'), may hold values from 0 to 17.5, as said below
- observations: float32 [16384], P('row'), may hold values from -6 to 6
Outputs:
- updated: float32 [16384, 16384], P('row', 'col')
- factor: float32 [16384, 256], P('row')
- whitened: float32 [16384], P('row')
Inputs may be any that keep to these rules, and one draw needn't show every extreme that they name: covariance rearranged to global order is symmetric and positive definite with every eigenvalue at least 0.5.
All inputs are finite; a program needn't handle non-finite values.
Results may differ from a plain program's by a relative error of at most 0.00019.
Values sent between devices are 32-bit elements; how exact they have to be, the bound alone decides.
A program may use at most 128 MiB of HBM per device.

v0:
```python
import jax
import jax.numpy as jnp
from jax import lax
from jax.sharding import PartitionSpec as P

TILE = 128


HIGH = lax.Precision.HIGHEST


def spread(block, axis, source):
    block = jnp.where(lax.axis_index(axis) == source, block, jnp.zeros_like(block))
    return lax.psum(block, axis)


def first_panel(rows, diag_one):
    tile = diag_one.shape[0]
    return jax.scipy.linalg.solve_triangular(diag_one, rows[:, :tile].T, lower=True).T


def second_panel(rows, first_col, below_one):
    tile = below_one.shape[0]
    return rows[:, tile : 2 * tile] - jnp.dot(
        first_col, below_one.T, precision=HIGH, preferred_element_type=jnp.float32
    )


def leading_factor(block):
    tile = block.shape[1] // 2
    diag_one = jnp.linalg.cholesky(block[:tile, :tile])
    first_col = first_panel(block, diag_one).at[:tile].set(diag_one)
    below_one = first_col[tile : 2 * tile]
    residue = second_panel(block, first_col, below_one)
    diag_two = jnp.linalg.cholesky(residue[tile : 2 * tile])
    second_col = jax.scipy.linalg.solve_triangular(diag_two, residue.T, lower=True).T
    second_col = (
        second_col.at[:tile]
        .set(jnp.zeros((tile, tile), jnp.float32))
        .at[tile : 2 * tile]
        .set(diag_two)
    )
    return (jnp.concatenate([first_col, second_col], 1), diag_one, below_one, diag_two)


def panel_rows(rows, diag_one, below_one, diag_two):
    first_col = first_panel(rows, diag_one)
    residue = second_panel(rows, first_col, below_one)
    second_col = jax.scipy.linalg.solve_triangular(diag_two, residue.T, lower=True).T
    return jnp.concatenate([first_col, second_col], 1)


def pick_tiles(block, col_tiles, groups, which):
    shaped = block.reshape(col_tiles, groups, TILE, 2 * TILE)
    return lax.dynamic_index_in_dim(shaped, which, 1, keepdims=False).reshape(
        col_tiles * TILE, 2 * TILE
    )


def per_device(covariance, observations):
    n_rows = lax.axis_size("row")
    n_cols = lax.axis_size("col")
    my_row = lax.axis_index("row")
    my_col = lax.axis_index("col")
    first_cols = covariance[:, :TILE]
    panel_first = spread(first_cols, "col", 0)
    panel_second = spread(first_cols, "col", 1)
    panels = jnp.concatenate([panel_first, panel_second], 1)
    lead_rows, lead_obs = (
        lax.all_gather(panels[:TILE], "row", axis=0, tiled=True),
        lax.all_gather(observations[:TILE], "row", axis=0, tiled=True),
    )
    lead, diag_one, below_one, diag_two = leading_factor(lead_rows[: 2 * TILE])
    lower = panel_rows(panels, diag_one, below_one, diag_two)
    offset_rows = jnp.minimum(my_row, 2) * TILE
    padded_lead = jnp.concatenate([lead, jnp.zeros((TILE, 2 * TILE), jnp.float32)], 0)
    first_tile = jnp.where(
        my_row < 2, lax.dynamic_slice_in_dim(padded_lead, offset_rows, TILE, 0), lower[:TILE]
    )
    factor = lower.at[:TILE].set(first_tile)
    solved = jax.scipy.linalg.solve_triangular(lead, lead_obs[: 2 * TILE], lower=True)
    white = observations - jnp.dot(
        factor, solved, precision=HIGH, preferred_element_type=jnp.float32
    )
    padded_solved = jnp.concatenate([solved, jnp.zeros((TILE,), jnp.float32)], 0)
    white_head = jnp.where(
        my_row < 2, lax.dynamic_slice_in_dim(padded_solved, offset_rows, TILE, 0), white[:TILE]
    )
    white = white.at[:TILE].set(white_head)
    groups = n_cols // n_rows
    col_tiles = covariance.shape[1] // TILE
    owner = my_col % n_rows
    which = my_col // n_rows
    own_tiles = pick_tiles(factor, col_tiles, groups, which)
    picked = spread(own_tiles, "row", owner)
    product = lax.dot_general(
        factor, picked, (((1,), (1,)), ((), ())), precision=HIGH, preferred_element_type=jnp.float32
    )
    return (covariance - product, factor, white)


def solution(mesh):
    placed = (P("row", "col"), P("row"))
    return jax.shard_map(
        per_device,
        mesh=mesh,
        in_specs=placed,
        out_specs=(P("row", "col"), P("row", None), P("row")),
        check_vma=False,
    )
```

profile of v0, /device:TPU:16, one launch (start us, length us, event | category | flops | bytes accessed | tf_op | source)
XLA Modules:
  0.0 357.8 jit_solution(11092610641022139542)
XLA Ops:
  7.2 1.2 slice-done
  8.7 1.6 broadcast_select_fusion.2
  10.4 159.1 %all-reduce.8.cloned.1.call-done = (f32[2048,128]{0,1:T(8,128)}, f32[2048,128]{0,1:T(8,128)}) async-done(((f32[2048,128]{0,1:T(8,128)}, f32[2048,128]{0,1:T(8,128)}), (f32[2048,128]{0,1:T(8,128)}, f32[2048,128]{0,1:T(8,128)})) %all-reduce.8.cloned.1.call-update) | async-done | bytes 2097168 | tf_op jit(solution)/shard_map/psum | solution.py:14
  169.4 1.6 pad_maximum_fusion.2
  171.2 8.1 %all-gather = f32[8,1,128]{2,1,0:T(1,128)S(1)} all-gather(f32[1,1,128]{2,1,0:T(1,128)S(1)} %slice_bitcast_fusion.9), channel_id=1, replica_groups=mesh['row'=8,'col'=32] {'row'}, dimensions={0}, use_global_device_ids=true | all-gather | bytes 4608 | tf_op jit(solution)/shard_map/all_gather | solution.py:71
  179.3 15.4 %all-gather.3.cloned.1.call-done = f32[1024,256]{0,1:T(8,128)} async-done(((f32[128,256]{0,1:T(8,128)}), f32[1024,256]{0,1:T(8,128)}) %all-gather.3.cloned.1.call-update) | async-done | bytes 1048592 | tf_op jit(solution)/shard_map/all_gather | solution.py:70
  196.5 11.7 %cholesky.44 = f32[128,128]{1,0:T(8,128)S(1)} custom-call(f32[128,128]{1,0:T(8,128)S(1)} %fusion.17), custom_call_target="Cholesky" | custom-call | tf_op jit(solution)/shard_map/jit(cholesky)/cholesky | solution.py:31
  209.5 9.8 %custom-call.15 = f32[1,128,128]{1,2,0:T(8,128)S(1)} custom-call(f32[1,128,128]{2,1,0:T(8,128)S(1)} %get-tuple-element.100), custom_call_target="InvertDiagBlocksLowerTriangular" | custom-call | tf_op jit(solution)/shard_map/jit(_solve_triangular)/triangular_solve | solution.py:19
  219.5 1.1 fusion.3
  220.5 1.2 convolution_bitcast_fusion.2
  221.8 1.2 convolution_subtract_fusion.2
  223.1 11.7 %cholesky.55 = f32[128,128]{1,0:T(8,128)S(1)} custom-call(f32[128,128]{1,0:T(8,128)S(1)} %fusion.14), custom_call_target="Cholesky" | custom-call | tf_op jit(solution)/shard_map/jit(cholesky)/cholesky | solution.py:35
  236.2 9.9 %custom-call.17 = f32[1,128,128]{1,2,0:T(8,128)S(1)} custom-call(f32[1,128,128]{2,1,0:T(8,128)S(1)} %get-tuple-element.98), custom_call_target="InvertDiagBlocksLowerTriangular" | custom-call | tf_op jit(solution)/shard_map/jit(_solve_triangular)/triangular_solve | solution.py:49
  246.7 4.2 %while.6 = (s32[]{:T(128)}, f32[256,256]{0,1:T(8,128)S(1)}, s32[2,2]{1,0:T(2,128)S(1)}, f32[2,128,128]{2,1,0:T(8,128)S(1)}, s32[]{:T(128)}) while((s32[]{:T(128)}, f32[256,256]{0,1:T(8,128)S(1)}, s32[2,2]{1,0:T(2,128)S(1)}, f32[2,128,128]{2,1,0:T(8,128)S(1)}, s32[]{:T(128)}) %tuple.54), condition=%wide.while_cond.5, body=%wide.while_body.5.sunk | while | flops 2 | bytes 393321 | solution.py:81
  247.2 1.4 dynamic-slice.47
  249.4 1.4 dynamic-slice.47
  250.9 19.7 %custom-call.12 = f32[2,128,128]{1,2,0:T(8,128)S(1)} custom-call(f32[2,128,128]{2,1,0:T(8,128)S(1)} %get-tuple-element.73), custom_call_target="InvertDiagBlocksLowerTriangular" | custom-call | tf_op jit(solution)/shard_map/jit(_solve_triangular)/triangular_solve | solution.py:81
  271.1 1.1 fusion
  273.4 2.4 reshape.156
  275.9 1.2 fusion.21
  277.1 3.3 fusion.5
  281.2 1.8 copy.20
  283.1 61.5 %all-reduce.6.cloned.1.call-done = f32[512,256]{0,1:T(8,128)} async-done(((f32[512,256]{0,1:T(8,128)}), f32[512,256]{0,1:T(8,128)}) %all-reduce.6.cloned.1.call-update) | async-done | bytes 524304 | tf_op jit(solution)/shard_map/psum | solution.py:14
  344.6 6.7 %convolution_subtract_fusion = f32[2048,512]{1,0:T(8,128)} fusion(f32[2048,512]{1,0:T(8,128)} %param.17, f32[2048,256]{0,1:T(8,128)S(1)} %fusion.9, f32[512,256]{0,1:T(8,128)} %all-reduce.6.cloned.1.call-done), kind=kOutput, calls=%fused_computation.2 | convolution fusion | flops 3222274048 | bytes 11010048 | tf_op jit(solution)/shard_map/dot_general | solution.py:96
  (57 shorter events, 9.7 us)
Async XLA Ops:
  7.2 1.2 slice-start
  7.2 162.2 %all-reduce.8.cloned.1.call-start = ((), (), s32[]{:S(2)}) async-start(), calls=%async_computation.2 | async-start | bytes 4194304 | tf_op jit(solution)/shard_map/psum | solution.py:14
  10.3 160.9 %copy-start.3 = (f32[2048]{0:T(1024)S(1)}, f32[2048]{0:T(1024)}, u32[]{:S(2)}) copy-start(f32[2048]{0:T(1024)} %param.18) | copy-start | bytes 24580
  10.3 184.4 %all-gather.3.cloned.1.call-start = ((), (), s32[]{:S(2)}) async-start(), calls=%async_computation | async-start | bytes 1179648 | tf_op jit(solution)/shard_map/all_gather | solution.py:70
  169.4 50.0 %copy-start.1 = (f32[2048,128]{0,1:T(8,128)S(1)}, f32[2048,128]{0,1:T(8,128)}, u32[]{:S(2)}) copy-start(f32[2048,128]{0,1:T(8,128)} %get-tuple-element.97) | copy-start | bytes 3145732
  171.1 173.5 %all-reduce.6.cloned.1.call-start = ((), (), s32[]{:S(2)}) async-start(), calls=%async_computation.1 | async-start | bytes 1048576 | tf_op jit(solution)/shard_map/psum | solution.py:14
  223.1 48.0 %copy-start = (f32[2048,128]{0,1:T(8,128)S(1)}, f32[2048,128]{0,1:T(8,128)}, u32[]{:S(2)}) copy-start(f32[2048,128]{0,1:T(8,128)} %get-tuple-element.96) | copy-start | bytes 3145732
  283.1 68.2 %copy-start.2 = (f32[2048]{0:T(1024)}, f32[2048]{0:T(1024)S(1)}, u32[]{:S(2)}) copy-start(f32[2048]{0:T(1024)S(1)} %constant_dynamic-update-slice_fusion) | copy-start | bytes 24580
Sparse Core Ops, SparseCore 0:
  12.2 157.1 all-reduce.7
  172.0 22.6 all-gather.2
  281.3 63.2 all-reduce.5
where the time goes:
time: 362 us; the launch traced here: 358 us
  waiting for transfers between devices  236 us (65%)
  other arithmetic  73.1 us (20%)
  matrix products  14.3 us (4%)
  between operations  14.1 us (4%)
  local copies, waits for them, and re-layouts  12 us (3%)
  blocking collectives  8.12 us (2%)
    psum x2, waiting for transfers between devices, spread(): return lax.psum(block, axis)  221 us
    another operation x4, other arithmetic, per_device(): jax.scipy.linalg.solve_triangular(lead, lead_obs[:2 * TILE], lower=True)  19.7 us
    all_gather x1, waiting for transfers between devices, per_device(): lax.all_gather(panels[:TILE], 'row', axis=0, tiled=True)  15.4 us
    another operation x3, other arithmetic, leading_factor(): diag_one = jnp.linalg.cholesky(block[:tile, :tile])  12.4 us
    another operation x3, other arithmetic, leading_factor(): diag_two = jnp.linalg.cholesky(residue[tile:2 * tile])  12.4 us
    another operation x2, other arithmetic, panel_rows(): jax.scipy.linalg.solve_triangular(diag_two, residue.T, lower=True)  10.6 us
    another operation x2, other arithmetic, first_panel(): jax.scipy.linalg.solve_triangular(diag_one, rows[:, :tile].T, lower=True)  10.5 us
    all_gather x1, blocking collectives, per_device(): lax.all_gather(observations[:TILE], 'row', axis=0, tiled=True)  8.12 us
  transfers between devices with their start and end apart: 3, of which 3 were waited for; matrix products, arithmetic and copies ran while one was open for 1% of the time, Pallas kernels for 0%

commit v1 on v0

v1 whole, which is shorter than its diff:
```python
import jax
import jax.numpy as jnp
from jax import lax
from jax.experimental import pallas as pl
from jax.experimental.pallas import tpu as pltpu
from jax.sharding import PartitionSpec as P

MESH = pl.DeviceIdType.MESH
TILE = 128
PANEL = 2 * TILE
NB = 16
N_ROW, N_COL, NX, NZ = 8, 32, 4, 8
CHUNK = 64
ALPHA = 16
SLICE = TILE // NZ
F32, BF16 = jnp.float32, jnp.bfloat16


def split3(x):
    high = x.astype(BF16)
    rest = x - high.astype(F32)
    mid = rest.astype(BF16)
    return high, mid, (rest - mid.astype(F32)).astype(BF16)


def split2(x):
    high = x.astype(BF16)
    return high, (x - high.astype(F32)).astype(BF16)


def mul(a, b, dims):
    return lax.dot_general(a, b, (dims, ((), ())), preferred_element_type=F32)


def mul6(a, b, dims):
    ah, am, al = split3(a)
    bh, bm, bl = split3(b)
    small = mul(ah, bl, dims) + mul(al, bh, dims) + mul(am, bm, dims)
    return small + (mul(ah, bm, dims) + mul(am, bh, dims)) + mul(ah, bh, dims)


NN, NT, TN = ((1,), (0,)), ((1,), (1,)), ((0,), (0,))


def triangle(x, keep_lower):
    r = lax.broadcasted_iota(jnp.int32, (TILE, TILE), 0)
    c = lax.broadcasted_iota(jnp.int32, (TILE, TILE), 1)
    return jnp.where(r >= c if keep_lower else r <= c, x, 0.0)


def init_work(work, block):
    r = lax.broadcasted_iota(jnp.int32, (TILE, TILE), 0)
    c = lax.broadcasted_iota(jnp.int32, (TILE, TILE), 1)
    work[:, :TILE] = block
    work[:, TILE:] = jnp.where(r == c, 1.0, 0.0).astype(F32)


def eliminate(g, work):
    base = g * NB
    here = pl.ds(pl.multiple_of(base, NB), NB)
    rows = work[here, :]
    turned = pltpu.roll(rows[:, :TILE], lax.rem(TILE - base, TILE), 1)
    cols = [jnp.broadcast_to(turned[:, j : j + 1], (NB, TILE)) for j in range(NB)]
    el = [[jnp.broadcast_to(cols[j][i : i + 1, :], (8, TILE)) for j in range(i + 1)] for i in range(NB)]
    left = [jnp.broadcast_to(rows[i : i + 1, :TILE], (8, TILE)) for i in range(NB)]
    right = [jnp.broadcast_to(rows[i : i + 1, TILE:], (8, TILE)) for i in range(NB)]
    for j in range(NB):
        inv = lax.rsqrt(el[j][j])
        left[j] = left[j] * inv
        right[j] = right[j] * inv
        low = [None] * NB
        for i in range(j + 1, NB):
            low[i] = el[i][j] * inv
        for i in range(j + 1, NB):
            for k in range(j + 1, i + 1):
                el[i][k] = el[i][k] - low[i] * low[k]
            left[i] = left[i] - low[i] * left[j]
            right[i] = right[i] - low[i] * right[j]
    sub = lax.broadcasted_iota(jnp.int32, (8, TILE), 0)

    def pack(parts):
        halves = []
        for h in range(NB // 8):
            acc = parts[h * 8]
            for i in range(1, 8):
                acc = jnp.where(sub == i, parts[h * 8 + i], acc)
            halves.append(acc)
        return jnp.concatenate(halves, 0)

    u_left, u_right = pack(left), pack(right)
    lane = lax.broadcasted_iota(jnp.int32, (NB, TILE), 1)
    below = jnp.where(lane >= base + NB, u_left, 0.0)
    u = jnp.concatenate([u_left, u_right], 1)
    h, m, l = split3(u)
    hb, mb, lb = split3(below)
    lhs = jnp.concatenate([hb, hb, mb, mb, hb, lb], 0)
    rhs = jnp.concatenate([h, m, h, m, l, h], 0)
    work[...] = work[...] - mul(lhs, rhs, TN)
    work[here, :] = u


def gather_kernel(
    cov, obs, pan, cols, heads, lead_out, inv_out,
    lead, turn, work, saved,
    load_sem, l1_send, l1_recv, l2_send, l2_recv, l3_send, l3_recv, sib_send, sib_recv,
    sc_send, sc_recv, z_send, z_recv, x_send, x_recv, a_send, a_recv, b_send, b_recv,
    c_send, c_recv, h_send, h_recv,
):
    r, c = lax.axis_index("row"), lax.axis_index("col")
    y, k = r // 2, r % 2
    x, z = c // NZ, c % NZ
    sib = r + 1 - 2 * k

    def dev(rr, cc):
        return {"row": rr, "col": cc}

    def x_peer(i):
        return ((x + i) % NX) * NZ + z

    def z_peer(i):
        return x * NZ + (z + i) % NZ

    def remote(src, dst, send, recv, rr, cc):
        return pltpu.make_async_remote_copy(
            src_ref=src, dst_ref=dst, send_sem=send, recv_sem=recv, device_id=dev(rr, cc), device_id_type=MESH
        )

    at_source = r < 2
    in_root_plane = c < NZ

    @pl.when(at_source)
    def _():
        pltpu.make_async_copy(cov.at[0:TILE, :], saved, load_sem.at[0]).start()

    barrier = pltpu.get_barrier_semaphore()

    def hello(rr, cc):
        pl.semaphore_signal(barrier, inc=1, device_id=dev(rr, cc), device_id_type=MESH)

    for i in range(1, NX):
        hello(r, x_peer(i))
    for i in range(1, NZ):
        hello(r, z_peer(i))
    for i in range(1, 4):
        hello((r + 2 * i) % N_ROW, c)
    hello(sib, c)
    hello(0, x * NZ + r)
    hello(1, x * NZ + r)
    hello(k, z)
    due = 14 + jnp.where(at_source, NZ, 0) + jnp.where(at_source & in_root_plane, 16, 0)
    pl.semaphore_wait(barrier, due)

    def level_one(block, owner):
        for i in range(NZ):
            rows = slice(SLICE * i, SLICE * (i + 1))

            @pl.when(z != i)
            def _():
                remote(
                    cov.at[rows, 0:TILE], lead.at[i, block], l1_send.at[i], l1_recv.at[block], r, i
                ).start()

            @pl.when(z == i)
            def _():
                pltpu.make_async_copy(cov.at[rows, 0:TILE], lead.at[i, block], l1_recv.at[block]).start()

    @pl.when((r == 0) & (c == 0))
    def _():
        level_one(0, 0)

    @pl.when((r == 1) & (c == 0))
    def _():
        level_one(1, 0)

    @pl.when((r == 1) & (c == 1))
    def _():
        level_one(2, 1)

    def wait_bytes(ref, sem):
        pltpu.make_async_copy(ref, ref, sem).wait()

    def mine(kk):
        return lead.at[z, 0:1] if kk == 0 else lead.at[z, 1:3]

    for kk in range(2):

        @pl.when((r == kk) & in_root_plane)
        def _():
            if kk == 0:
                wait_bytes(lead.at[z, 0], l1_recv.at[0])
            else:
                wait_bytes(lead.at[z, 1], l1_recv.at[1])
                wait_bytes(lead.at[z, 2], l1_recv.at[2])
            for yy in range(4):
                for xx in range(NX):
                    if (yy, xx) != (0, 0):
                        remote(
                            mine(kk), mine(kk), l2_send.at[yy * NX + xx], l2_recv, 2 * yy + kk, xx * NZ + z
                        ).start()

    is_root_line = at_source & in_root_plane
    for kk in range(2):

        @pl.when(k == kk)
        def _():
            @pl.when(jnp.logical_not(is_root_line))
            def _():
                wait_bytes(mine(kk), l2_recv)

            for i in range(1, NZ):
                remote(mine(kk), mine(kk), l3_send.at[i], l3_recv.at[z], r, z_peer(i)).start()

    @pl.when(at_source)
    def _():
        pltpu.make_async_copy(cov.at[0:TILE, :], saved, load_sem.at[0]).wait()
        for s in range(4):
            turn[s] = saved[:, s * TILE : (s + 1) * TILE].T
        for kk in range(2):

            @pl.when(r == kk)
            def _():
                for i in range(NZ):
                    src = turn.at[i // 2, CHUNK * (i % 2) : CHUNK * (i % 2 + 1), :]
                    dst = pan.at[i // 2, x, i % 2, :, kk * TILE : (kk + 1) * TILE]

                    @pl.when((z == kk) & (z == i))
                    def _():
                        pltpu.make_async_copy(src, dst, sc_recv.at[kk]).start()

                    @pl.when(jnp.logical_not((z == kk) & (z == i)))
                    def _():
                        remote(src, dst, sc_send.at[i], sc_recv.at[kk], z, x * NZ + i).start()

    for kk in range(2):

        @pl.when(r == kk)
        def _():
            pltpu.make_async_copy(cov.at[0:TILE, :], cols.at[kk], c_recv.at[0]).start()
            pltpu.make_async_copy(obs.at[0:8, :], heads.at[kk], h_recv.at[0]).start()
            for i in range(1, 4):
                rr = (r + 2 * i) % N_ROW
                remote(cov.at[0:TILE, :], cols.at[kk], c_send.at[i], c_recv.at[0], rr, c).start()
                remote(obs.at[0:8, :], heads.at[kk], h_send.at[i], h_recv.at[0], rr, c).start()

    def gathered(kk, zz):
        return lead.at[zz, 0:1] if kk == 0 else lead.at[zz, 1:3]

    def whole(kk):
        return lead.at[:, 0:1] if kk == 0 else lead.at[:, 1:3]

    for kk in range(2):

        @pl.when(k == kk)
        def _():
            for i in range(1, NZ):
                zz = (z + i) % NZ
                wait_bytes(gathered(kk, zz), l3_recv.at[zz])
            remote(whole(kk), whole(kk), sib_send, sib_recv, sib, c).start()

    own = pan.at[z // 2, x, z % 2]
    for kk in range(2):
        wait_bytes(pan.at[z // 2, x, z % 2, :, kk * TILE : (kk + 1) * TILE], sc_recv.at[kk])
    for i in range(1, NX):
        remote(own, own, x_send.at[i], x_recv.at[x], r, x_peer(i)).start()
    for i in range(1, NZ):
        remote(own, own, z_send.at[i], z_recv.at[z], r, z_peer(i)).start()

    def forward_x(i):
        xx = (x + i) % NX
        wait_bytes(pan.at[z // 2, xx, z % 2], x_recv.at[xx])
        part = pan.at[z // 2, xx, z % 2, 0:ALPHA, :]
        for j in range(1, NZ):
            remote(part, part, a_send.at[i, j], a_recv.at[xx, z], r, z_peer(j)).start()

    def forward_z(i):
        zz = (z + i) % NZ
        wait_bytes(pan.at[zz // 2, x, zz % 2], z_recv.at[zz])
        part = pan.at[zz // 2, x, zz % 2, ALPHA:CHUNK, :]
        for j in range(1, NX):
            remote(part, part, b_send.at[i, j], b_recv.at[x, zz], r, x_peer(j)).start()

    for kk in range(2):

        @pl.when(k != kk)
        def _():
            wait_bytes(whole(kk), sib_recv)

    def block(b):
        return lead[:, b].reshape(TILE, TILE)

    init_work(work, block(0))

    def first(g, _):
        eliminate(g, work)

        @pl.when((g >= 0) & (g < 3))
        def _():
            forward_x(g + 1)

        @pl.when((g >= 1) & (g < 8))
        def _():
            n = g - 1
            forward_z(jnp.where(n % 2 == 0, n // 2 + 1, NZ - 1 - n // 2))

        return 0

    lax.fori_loop(0, TILE // NB, first, 0)
    diag_t = triangle(work[:, :TILE], False)
    inv_one = triangle(work[:, TILE:], True)
    lead_out[0:TILE, 0:TILE] = diag_t.T
    lead_out[0:TILE, TILE:PANEL] = jnp.zeros((TILE, TILE), F32)
    inv_out[0:TILE, 0:TILE] = inv_one
    inv_out[0:TILE, TILE:PANEL] = jnp.zeros((TILE, TILE), F32)
    below = mul6(block(1), inv_one, NT)
    lead_out[TILE:PANEL, 0:TILE] = below
    init_work(work, block(2) - mul6(below, below, NT))
    joint = mul6(below, inv_one, NN)

    for kk in range(2):

        @pl.when(k == kk)
        def _():
            wait_bytes(cols.at[kk], c_recv.at[0])
            wait_bytes(heads.at[kk], h_recv.at[0])
            remote(cols.at[kk], cols.at[kk], c_send.at[0], c_recv.at[1], sib, c).start()
            remote(heads.at[kk], heads.at[kk], h_send.at[0], h_recv.at[1], sib, c).start()

    def second(g, _):
        eliminate(g, work)
        return 0

    lax.fori_loop(0, TILE // NB, second, 0)
    inv_two = triangle(work[:, TILE:], True)
    lead_out[TILE:PANEL, TILE:PANEL] = triangle(work[:, :TILE], False).T
    inv_out[TILE:PANEL, TILE:PANEL] = inv_two
    inv_out[TILE:PANEL, 0:TILE] = -mul6(inv_two, joint, NN)

    for kk in range(2):

        @pl.when(k != kk)
        def _():
            wait_bytes(cols.at[kk], c_recv.at[1])
            wait_bytes(heads.at[kk], h_recv.at[1])

    for i in range(1, NX):
        xx = (x + i) % NX
        for j in range(1, NZ):
            zz = (z + j) % NZ
            wait_bytes(pan.at[zz // 2, xx, zz % 2, 0:ALPHA, :], a_recv.at[xx, zz])
            wait_bytes(pan.at[zz // 2, xx, zz % 2, ALPHA:CHUNK, :], b_recv.at[xx, zz])

    for i in range(1, NX):
        wait_bytes(own, x_send.at[i])
        for j in range(1, NZ):
            wait_bytes(pan.at[z // 2, 0, z % 2, 0:ALPHA, :], a_send.at[i, j])
    for i in range(1, NZ):
        wait_bytes(own, z_send.at[i])
        for j in range(1, NX):
            wait_bytes(pan.at[0, x, 0, ALPHA:CHUNK, :], b_send.at[i, j])
    for kk in range(2):

        @pl.when(k == kk)
        def _():
            for i in range(1, NZ):
                wait_bytes(mine(kk), l3_send.at[i])
            wait_bytes(whole(kk), sib_send)
            wait_bytes(cols.at[kk], c_send.at[0])
            wait_bytes(heads.at[kk], h_send.at[0])

        @pl.when(r == kk)
        def _():
            for i in range(1, 4):
                wait_bytes(cols.at[kk], c_send.at[i])
                wait_bytes(heads.at[kk], h_send.at[i])
            for i in range(NZ):

                @pl.when(jnp.logical_not((z == kk) & (z == i)))
                def _():
                    wait_bytes(turn.at[0, 0:CHUNK, :], sc_send.at[i])

        @pl.when((r == kk) & in_root_plane)
        def _():
            for i in range(1, 16):
                wait_bytes(mine(kk), l2_send.at[i])

    @pl.when(((r < 2) & (c == 0)) | ((r == 1) & (c == 1)))
    def _():
        for i in range(NZ):

            @pl.when(z != i)
            def _():
                wait_bytes(lead.at[0, 0], l1_send.at[i])


def update_kernel(cov, pan, obs, cols, heads, lead, inv, out, fac, white, inv_t, col_h, col_l, z_rows):
    step = pl.program_id(0)
    r = lax.axis_index("row")
    n = fac.shape[0]

    @pl.when(step == 0)
    def _():
        h, m, l = split3(inv[...].T)
        inv_t[0], inv_t[1], inv_t[2] = h, m, l
        h, l = split2(mul6(inv[...], cols[...], NN))
        col_h[...], col_l[...] = h, l
        first = jnp.concatenate([heads[0, 0:1, :], heads[1, 0:1, :]], 1)
        z_rows[...] = mul6(jnp.broadcast_to(first, (8, PANEL)), inv[...], NT)

    p_h, p_m, p_l = split3(pan[...])
    small = mul(p_h, inv_t[2], NN) + mul(p_l, inv_t[0], NN) + mul(p_m, inv_t[1], NN)
    rows = small + (mul(p_h, inv_t[1], NN) + mul(p_m, inv_t[0], NN)) + mul(p_h, inv_t[0], NN)
    fac[...] = rows

    @pl.when((step == 0) & (r < 2))
    def _():
        fac[0:TILE, :] = lead[pl.ds(pl.multiple_of(jnp.minimum(r, 1) * TILE, TILE), TILE), :]

    rows = fac[...]
    f_h, f_l = split2(rows)
    out[...] = cov[...] - (mul(f_h, col_l[...], NN) + mul(f_l, col_h[...], NN) + mul(f_h, col_h[...], NN))
    shift = mul6(z_rows[...], rows, NT)[0:1, :]
    for j in range(n // TILE):
        at = pl.ds(step * (n // TILE) + j, 1)
        white[at, :] = obs[at, :] - shift[:, j * TILE : (j + 1) * TILE]

    @pl.when((step == 0) & (r == 0))
    def _():
        white[0:1, :] = z_rows[0:1, 0:TILE]

    @pl.when((step == 0) & (r == 1))
    def _():
        white[0:1, :] = z_rows[0:1, TILE:PANEL]


def per_device(covariance, observations):
    obs = observations.reshape(16, TILE)
    dma = pltpu.SemaphoreType.DMA
    hbm = pl.BlockSpec(memory_space=pl.ANY)
    vmem = pl.BlockSpec(memory_space=pltpu.VMEM)
    pan, cols, heads, lead, inv = pl.pallas_call(
        gather_kernel,
        out_shape=[
            jax.ShapeDtypeStruct((4, NX, 2, CHUNK, PANEL), F32),
            jax.ShapeDtypeStruct((2, TILE, 512), F32),
            jax.ShapeDtypeStruct((2, 8, TILE), F32),
            jax.ShapeDtypeStruct((PANEL, PANEL), F32),
            jax.ShapeDtypeStruct((PANEL, PANEL), F32),
        ],
        in_specs=[hbm, hbm],
        out_specs=[hbm, hbm, hbm, vmem, vmem],
        scratch_shapes=[
            pltpu.VMEM((NZ, 3, SLICE, TILE), F32),
            pltpu.VMEM((4, TILE, TILE), F32),
            pltpu.VMEM((TILE, PANEL), F32),
            pltpu.VMEM((TILE, 512), F32),
            dma((1,)),
            dma((8,)), dma((3,)), dma((16,)), dma, dma((8,)), dma((8,)), dma, dma,
            dma((8,)), dma((2,)), dma((8,)), dma((8,)), dma((4,)), dma((4,)),
            dma((4, 8)), dma((4, 8)), dma((8, 4)), dma((4, 8)),
            dma((4,)), dma((2,)), dma((4,)), dma((2,)),
        ],
        compiler_params=pltpu.CompilerParams(collective_id=0, has_side_effects=True, vmem_limit_bytes=32 << 20),
    )(covariance, obs)
    rows = 256
    fixed = lambda *shape: pl.BlockSpec(shape, lambda i: (0,) * len(shape))
    out, fac, white = pl.pallas_call(
        update_kernel,
        grid=(2048 // rows,),
        out_shape=[
            jax.ShapeDtypeStruct((2048, 512), F32),
            jax.ShapeDtypeStruct((2048, PANEL), F32),
            jax.ShapeDtypeStruct((16, TILE), F32),
        ],
        in_specs=[
            pl.BlockSpec((rows, 512), lambda i: (i, 0)),
            pl.BlockSpec((rows, PANEL), lambda i: (i, 0)),
            fixed(16, TILE),
            fixed(PANEL, 512),
            fixed(2, 8, TILE),
            fixed(PANEL, PANEL),
            fixed(PANEL, PANEL),
        ],
        out_specs=[
            pl.BlockSpec((rows, 512), lambda i: (i, 0)),
            pl.BlockSpec((rows, PANEL), lambda i: (i, 0)),
            fixed(16, TILE),
        ],
        scratch_shapes=[
            pltpu.VMEM((3, PANEL, PANEL), BF16),
            pltpu.VMEM((PANEL, 512), BF16),
            pltpu.VMEM((PANEL, 512), BF16),
            pltpu.VMEM((8, PANEL), F32),
        ],
        compiler_params=pltpu.CompilerParams(vmem_limit_bytes=32 << 20),
    )(covariance, pan.reshape(2048, PANEL), obs, cols.reshape(PANEL, 512), heads, lead, inv)
    return out, fac, white.reshape(2048)


def solution(mesh):
    placed = (P("row", "col"), P("row"))
    return jax.shard_map(
        per_device,
        mesh=mesh,
        in_specs=placed,
        out_specs=(P("row", "col"), P("row", None), P("row")),
        check_vma=False,
    )
```

time: 362 us -> 70.1 us (0.19); the launches traced: 358 us -> 69.9 us
  waiting for transfers between devices: 236 us -> 0 us
  other arithmetic: 73.1 us -> 0 us
  Pallas kernels: 0 us -> 66.4 us
  matrix products: 14.3 us -> 0 us
  between operations: 14.1 us -> 0.65 us
  local copies, waits for them, and re-layouts: 12 us -> 2.88 us
  blocking collectives: 8.12 us -> 0 us
    psum x2 -> x0, waiting for transfers between devices: 221 us -> none  [spread(): return lax.psum(block, axis)]
    pallas_call x0 -> x2, Pallas kernels: none -> 66.4 us  [the longest x1 56.4 us: per_device(): pl.pallas_call(gather_kernel, out_shape=[jax.ShapeDtypeStruct((4, NX, 2,...]
    another operation x14 -> x0, other arithmetic: 65.5 us -> none  [the longest x4 19.7 us: per_device(): jax.scipy.linalg.solve_triangular(lead, lead_obs[:2 * TILE], lower=True)]
    all_gather x1 -> x0, waiting for transfers between devices: 15.4 us -> none  [per_device(): lax.all_gather(panels[:TILE], 'row', axis=0, tiled=True)]
    dot_general x4 -> x0, matrix products: 10.2 us -> none  [the longest x1 6.71 us: per_device(): lax.dot_general(factor, picked, (((1,), (1,)), ((), ())), precision=HIGH,...]
    all_gather x1 -> x0, blocking collectives: 8.12 us -> none  [per_device(): lax.all_gather(observations[:TILE], 'row', axis=0, tiled=True)]
    select_n x2 -> x0, other arithmetic: 4.84 us -> none  [spread(): jnp.where(lax.axis_index(axis) == source, block, jnp.zeros_like(block))]
    another operation x11 -> x0, local copies, waits for them, and re-layouts: 4.22 us -> none
  transfers between devices with their start and end apart: 3 -> 0, of which waited for: 3 -> 0; matrix products, arithmetic and copies ran while one was open for 1% -> 0% of each run, Pallas kernels for 0% -> 0%
where the time goes in v1:
time: 70.1 us; the launch traced here: 69.9 us
  Pallas kernels  66.4 us (95%)
  local copies, waits for them, and re-layouts  2.88 us (4%)
    pallas_call x1, Pallas kernels, per_device(): pl.pallas_call(gather_kernel, out_shape=[jax.ShapeDtypeStruct((4, NX, 2,...  56.4 us
    pallas_call x1, Pallas kernels, per_device(): pl.pallas_call(update_kernel, grid=(2048 // rows,), out_shape=[jax.ShapeD...  10 us
    unnamed x4, local copies, waits for them, and re-layouts  2.88 us

profile of v1, /device:TPU:16, one launch (start us, length us, event | category | flops | bytes accessed | tf_op | source)
XLA Modules:
  0.0 69.9 jit_solution(17938207618844655047)
XLA Ops:
  0.6 0.0 copy-start
  0.6 2.2 %copy-done = f32[2048,512]{1,0:T(8,128)S(1)} copy-done((f32[2048,512]{1,0:T(8,128)S(1)}, f32[2048,512]{1,0:T(8,128)}, u32[]{:S(2)}) %copy-start) | copy-done | bytes 4194328
  2.8 0.0 copy-start.1
  2.8 0.7 copy-done.1
  3.5 56.4 %shard_map.49 = (f32[4,4,2,64,256]{4,3,2,1,0:T(8,128)S(1)}, f32[2,128,512]{2,1,0:T(8,128)S(1)}, f32[2,8,128]{2,1,0:T(8,128)S(1)}, f32[256,256]{1,0:T(8,128)S(1)}, f32[256,256]{1,0:T(8,128)S(1)}) custom-call(f32[2048,512]{1,0:T(8,128)S(1)} %copy-done, f32[16,128]{1,0:T(8,128)S(1)} %bitcast.6), custom_call_target="tpu_custom_call" | custom-call | tf_op jit(solution)/shard_map/pallas_call | solution.py:440
  59.9 10.0 %shard_map.50 = (f32[2048,512]{1,0:T(8,128)}, f32[2048,256]{1,0:T(8,128)}, f32[16,128]{1,0:T(8,128)}) custom-call(f32[2048,512]{1,0:T(8,128)S(1)} %copy-done, f32[2048,256]{1,0:T(8,128)S(1)} %bitcast.4, f32[16,128]{1,0:T(8,128)S(1)} %bitcast.7, f32[256,512]{1,0:T(8,128)S(1)} %bitcast.5, f32[2,8,128]{2,1,0:T(8,128)S(1)} %get-tuple-element.13.heads, ...), custom_call_target="tpu_custom_call" | custom-call | tf_op jit(solution)/shard_map/pallas_call | solution.py:466
Async XLA Ops:
  0.6 2.2 %copy-start = (f32[2048,512]{1,0:T(8,128)S(1)}, f32[2048,512]{1,0:T(8,128)}, u32[]{:S(2)}) copy-start(f32[2048,512]{1,0:T(8,128)} %cov.3) | copy-start | bytes 12582916
  2.8 0.7 copy-start.1

commit v2 on v1

--- a/solution.py
+++ b/solution.py
@@ -11,7 +11,9 @@
 NB = 16
 N_ROW, N_COL, NX, NZ = 8, 32, 4, 8
 CHUNK = 64
-ALPHA = 16
+HALF = CHUNK // 2
+QUARTER = CHUNK // 4
+PARTS = 4
 SLICE = TILE // NZ
 F32, BF16 = jnp.float32, jnp.bfloat16
 
@@ -100,10 +102,10 @@
 
 
 def gather_kernel(
-    cov, obs, pan, cols, heads, lead_out, inv_out,
+    cov, obs, pan, cols, heads, inv_out, cov_here, obs_here,
     lead, turn, work, saved,
     load_sem, l1_send, l1_recv, l2_send, l2_recv, l3_send, l3_recv, sib_send, sib_recv,
-    sc_send, sc_recv, z_send, z_recv, x_send, x_recv, a_send, a_recv, b_send, b_recv,
+    sc_send, sc_recv, x_send, x_recv, up_send, up_recv, down_send, down_recv, side_send, side_recv,
     c_send, c_recv, h_send, h_recv,
 ):
     r, c = lax.axis_index("row"), lax.axis_index("col")
@@ -147,6 +149,12 @@
     hello(0, x * NZ + r)
     hello(1, x * NZ + r)
     hello(k, z)
+    @pl.when(at_source)
+    def _():
+        pltpu.make_async_copy(cov.at[0:TILE, :], saved, load_sem.at[0]).wait()
+        for s in range(4):
+            turn[s] = saved[:, s * TILE : (s + 1) * TILE].T
+
     due = 14 + jnp.where(at_source, NZ, 0) + jnp.where(at_source & in_root_plane, 16, 0)
     pl.semaphore_wait(barrier, due)
 
@@ -212,9 +220,6 @@
 
     @pl.when(at_source)
     def _():
-        pltpu.make_async_copy(cov.at[0:TILE, :], saved, load_sem.at[0]).wait()
-        for s in range(4):
-            turn[s] = saved[:, s * TILE : (s + 1) * TILE].T
         for kk in range(2):
 
             @pl.when(r == kk)
@@ -230,6 +235,58 @@
                     @pl.when(jnp.logical_not((z == kk) & (z == i)))
                     def _():
                         remote(src, dst, sc_send.at[i], sc_recv.at[kk], z, x * NZ + i).start()
+
+    own = pan.at[z // 2, x, z % 2]
+    for kk in range(2):
+        wait_bytes(pan.at[z // 2, x, z % 2, :, kk * TILE : (kk + 1) * TILE], sc_recv.at[kk])
+
+    def chunk(xx, zz, first, count):
+        return pan.at[zz // 2, xx, zz % 2, first : first + count, :]
+
+    def pass_on(i, d, first, count):
+        xx = (x + i) % NX
+        for way, send, recv in ((1, up_send, up_recv), (-1, down_send, down_recv)):
+            zz = (z - way * (d - 1) + NZ) % NZ
+            low, rows = first, count
+            if d == NZ // 2:
+                rows = count // 2
+                low = first if way == 1 else first + rows
+            part = chunk(xx, zz, low, rows)
+            remote(part, part, send.at[i, d], recv.at[i, d], r, x * NZ + (z + way + NZ) % NZ).start()
+
+    def landed(i, d, first, count):
+        xx = (x + i) % NX
+        for way, recv in ((1, up_recv), (-1, down_recv)):
+            zz = (z - way * d + NZ) % NZ
+            low, rows = first, count
+            if d == NZ // 2:
+                rows = count // 2
+                low = first if way == 1 else first + rows
+            wait_bytes(chunk(xx, zz, low, rows), recv.at[i, d])
+
+    def sideways(zz, d, way):
+        part = chunk(x, zz, HALF, HALF)
+        for j in range(1, NX):
+            remote(part, part, side_send.at[d, j], side_recv.at[zz, x], r, x_peer(j)).start()
+
+    def own_column(d):
+        landed(0, d, 0, CHUNK)
+        if d < NZ // 2:
+            pass_on(0, d + 1, 0, CHUNK)
+            sideways((z - d + NZ) % NZ, d, 1)
+            sideways((z + d) % NZ, NZ - d, -1)
+        else:
+            sideways((z + d) % NZ, d, -1)
+
+    def other_columns(d):
+        for i in range(1, NX):
+            landed(i, d, 0, HALF)
+            if d < NZ // 2:
+                pass_on(i, d + 1, 0, HALF)
+
+    pass_on(0, 1, 0, CHUNK)
+    for i in range(1, NX):
+        remote(own, own, x_send.at[i], x_recv.at[x], r, x_peer(i)).start()
 
     for kk in range(2):
 
@@ -242,6 +299,17 @@
                 remote(cov.at[0:TILE, :], cols.at[kk], c_send.at[i], c_recv.at[0], rr, c).start()
                 remote(obs.at[0:8, :], heads.at[kk], h_send.at[i], h_recv.at[0], rr, c).start()
 
+    load_cov = pltpu.make_async_copy(cov, cov_here, load_sem.at[1])
+    load_cov.start()
+    load_obs = pltpu.make_async_copy(obs, obs_here, load_sem.at[2])
+    load_obs.start()
+
+    own_column(1)
+    for i in range(1, NX):
+        xx = (x + i) % NX
+        wait_bytes(chunk(xx, z, 0, CHUNK), x_recv.at[xx])
+        pass_on(i, 1, 0, HALF)
+
     def gathered(kk, zz):
         return lead.at[zz, 0:1] if kk == 0 else lead.at[zz, 1:3]
 
@@ -257,28 +325,6 @@
                 wait_bytes(gathered(kk, zz), l3_recv.at[zz])
             remote(whole(kk), whole(kk), sib_send, sib_recv, sib, c).start()
 
-    own = pan.at[z // 2, x, z % 2]
-    for kk in range(2):
-        wait_bytes(pan.at[z // 2, x, z % 2, :, kk * TILE : (kk + 1) * TILE], sc_recv.at[kk])
-    for i in range(1, NX):
-        remote(own, own, x_send.at[i], x_recv.at[x], r, x_peer(i)).start()
-    for i in range(1, NZ):
-        remote(own, own, z_send.at[i], z_recv.at[z], r, z_peer(i)).start()
-
-    def forward_x(i):
-        xx = (x + i) % NX
-        wait_bytes(pan.at[z // 2, xx, z % 2], x_recv.at[xx])
-        part = pan.at[z // 2, xx, z % 2, 0:ALPHA, :]
-        for j in range(1, NZ):
-            remote(part, part, a_send.at[i, j], a_recv.at[xx, z], r, z_peer(j)).start()
-
-    def forward_z(i):
-        zz = (z + i) % NZ
-        wait_bytes(pan.at[zz // 2, x, zz % 2], z_recv.at[zz])
-        part = pan.at[zz // 2, x, zz % 2, ALPHA:CHUNK, :]
-        for j in range(1, NX):
-            remote(part, part, b_send.at[i, j], b_recv.at[x, zz], r, x_peer(j)).start()
-
     for kk in range(2):
 
         @pl.when(k != kk)
@@ -288,31 +334,30 @@
     def block(b):
         return lead[:, b].reshape(TILE, TILE)
 
+    FIRST = (
+        (1, lambda: own_column(2)),
+        (2, lambda: other_columns(1)),
+        (4, lambda: own_column(3)),
+        (6, lambda: other_columns(2)),
+    )
+    SECOND = ((0, lambda: own_column(4)), (2, lambda: other_columns(3)))
     init_work(work, block(0))
 
     def first(g, _):
         eliminate(g, work)
-
-        @pl.when((g >= 0) & (g < 3))
-        def _():
-            forward_x(g + 1)
-
-        @pl.when((g >= 1) & (g < 8))
-        def _():
-            n = g - 1
-            forward_z(jnp.where(n % 2 == 0, n // 2 + 1, NZ - 1 - n // 2))
+        for at, service in FIRST:
+
+            @pl.when(g == at)
+            def _():
+                service()
 
         return 0
 
     lax.fori_loop(0, TILE // NB, first, 0)
-    diag_t = triangle(work[:, :TILE], False)
     inv_one = triangle(work[:, TILE:], True)
-    lead_out[0:TILE, 0:TILE] = diag_t.T
-    lead_out[0:TILE, TILE:PANEL] = jnp.zeros((TILE, TILE), F32)
     inv_out[0:TILE, 0:TILE] = inv_one
     inv_out[0:TILE, TILE:PANEL] = jnp.zeros((TILE, TILE), F32)
     below = mul6(block(1), inv_one, NT)
-    lead_out[TILE:PANEL, 0:TILE] = below
     init_work(work, block(2) - mul6(below, below, NT))
     joint = mul6(below, inv_one, NN)
 
@@ -327,11 +372,16 @@
 
     def second(g, _):
         eliminate(g, work)
+        for at, service in SECOND:
+
+            @pl.when(g == at)
+            def _():
+                service()
+
         return 0
 
     lax.fori_loop(0, TILE // NB, second, 0)
     inv_two = triangle(work[:, TILE:], True)
-    lead_out[TILE:PANEL, TILE:PANEL] = triangle(work[:, :TILE], False).T
     inv_out[TILE:PANEL, TILE:PANEL] = inv_two
     inv_out[TILE:PANEL, 0:TILE] = -mul6(inv_two, joint, NN)
 
@@ -342,21 +392,25 @@
             wait_bytes(cols.at[kk], c_recv.at[1])
             wait_bytes(heads.at[kk], h_recv.at[1])
 
+    other_columns(NZ // 2)
     for i in range(1, NX):
         xx = (x + i) % NX
         for j in range(1, NZ):
             zz = (z + j) % NZ
-            wait_bytes(pan.at[zz // 2, xx, zz % 2, 0:ALPHA, :], a_recv.at[xx, zz])
-            wait_bytes(pan.at[zz // 2, xx, zz % 2, ALPHA:CHUNK, :], b_recv.at[xx, zz])
-
-    for i in range(1, NX):
-        wait_bytes(own, x_send.at[i])
-        for j in range(1, NZ):
-            wait_bytes(pan.at[z // 2, 0, z % 2, 0:ALPHA, :], a_send.at[i, j])
-    for i in range(1, NZ):
-        wait_bytes(own, z_send.at[i])
-        for j in range(1, NX):
-            wait_bytes(pan.at[0, x, 0, ALPHA:CHUNK, :], b_send.at[i, j])
+            wait_bytes(chunk(xx, zz, HALF, HALF), side_recv.at[zz, xx])
+    load_cov.wait()
+    load_obs.wait()
+
+    for i in range(NX):
+        rows = CHUNK if i == 0 else HALF
+        for d in range(1, NZ // 2 + 1):
+            part = chunk(x, z, 0, rows if d < NZ // 2 else rows // 2)
+            wait_bytes(part, up_send.at[i, d])
+            wait_bytes(part, down_send.at[i, d])
+    for j in range(1, NX):
+        wait_bytes(own, x_send.at[j])
+        for d in range(1, NZ):
+            wait_bytes(chunk(x, z, HALF, HALF), side_send.at[d, j])
     for kk in range(2):
 
         @pl.when(k == kk)
@@ -392,107 +446,103 @@
                 wait_bytes(lead.at[0, 0], l1_send.at[i])
 
 
-def update_kernel(cov, pan, obs, cols, heads, lead, inv, out, fac, white, inv_t, col_h, col_l, z_rows):
-    step = pl.program_id(0)
+def update_kernel(cov, pan, obs, cols, heads, inv, out, fac, white, rows, done, sems):
     r = lax.axis_index("row")
-    n = fac.shape[0]
-
-    @pl.when(step == 0)
-    def _():
-        h, m, l = split3(inv[...].T)
-        inv_t[0], inv_t[1], inv_t[2] = h, m, l
-        h, l = split2(mul6(inv[...], cols[...], NN))
-        col_h[...], col_l[...] = h, l
-        first = jnp.concatenate([heads[0, 0:1, :], heads[1, 0:1, :]], 1)
-        z_rows[...] = mul6(jnp.broadcast_to(first, (8, PANEL)), inv[...], NT)
-
+    h, m, l = split3(inv[...].T)
     p_h, p_m, p_l = split3(pan[...])
-    small = mul(p_h, inv_t[2], NN) + mul(p_l, inv_t[0], NN) + mul(p_m, inv_t[1], NN)
-    rows = small + (mul(p_h, inv_t[1], NN) + mul(p_m, inv_t[0], NN)) + mul(p_h, inv_t[0], NN)
-    fac[...] = rows
-
-    @pl.when((step == 0) & (r < 2))
-    def _():
-        fac[0:TILE, :] = lead[pl.ds(pl.multiple_of(jnp.minimum(r, 1) * TILE, TILE), TILE), :]
-
-    rows = fac[...]
-    f_h, f_l = split2(rows)
-    out[...] = cov[...] - (mul(f_h, col_l[...], NN) + mul(f_l, col_h[...], NN) + mul(f_h, col_h[...], NN))
-    shift = mul6(z_rows[...], rows, NT)[0:1, :]
-    for j in range(n // TILE):
-        at = pl.ds(step * (n // TILE) + j, 1)
-        white[at, :] = obs[at, :] - shift[:, j * TILE : (j + 1) * TILE]
-
-    @pl.when((step == 0) & (r == 0))
-    def _():
-        white[0:1, :] = z_rows[0:1, 0:TILE]
-
-    @pl.when((step == 0) & (r == 1))
-    def _():
-        white[0:1, :] = z_rows[0:1, TILE:PANEL]
+    small = mul(p_h, l, NN) + mul(p_l, h, NN) + mul(p_m, m, NN)
+    rows[...] = small + (mul(p_h, m, NN) + mul(p_m, h, NN)) + mul(p_h, h, NN)
+
+    @pl.when(r == 0)
+    def _():
+        rows[0:TILE, 0:TILE] = triangle(rows[0:TILE, 0:TILE], True)
+        rows[0:TILE, TILE:PANEL] = jnp.zeros((TILE, TILE), F32)
+
+    @pl.when(r == 1)
+    def _():
+        rows[0:TILE, TILE:PANEL] = triangle(rows[0:TILE, TILE:PANEL], True)
+
+    write_rows = pltpu.make_async_copy(rows, fac, sems.at[0])
+    write_rows.start()
+    c_h, c_l = split2(mul6(inv[...], cols[...], NN))
+    first = jnp.concatenate([heads[0, 0:1, :], heads[1, 0:1, :]], 1)
+    z_row = mul6(jnp.broadcast_to(first, (8, PANEL)), inv[...], NT)[0:1, :]
+    writes = []
+    for i in range(PARTS):
+        n = 2048 // PARTS
+        at = slice(i * n, (i + 1) * n)
+        f_h, f_l = split2(rows[at, :])
+        done[at, :] = cov[at, :] - (mul(f_h, c_l, NN) + mul(f_l, c_h, NN) + mul(f_h, c_h, NN))
+        copy = pltpu.make_async_copy(done.at[at, :], out.at[at, :], sems.at[1 + i])
+        copy.start()
+        writes.append(copy)
+    lane = lax.broadcasted_iota(jnp.int32, (TILE, TILE), 1)
+    acc = jnp.zeros((TILE, TILE), F32)
+    for t in range(16):
+        part = jnp.sum(rows[t * TILE : (t + 1) * TILE, :] * z_row, axis=1, keepdims=True)
+        acc = jnp.where(lane == t, part, acc)
+    white[...] = obs[...] - acc.T[0:16]
+
+    @pl.when(r == 0)
+    def _():
+        white[0:1, :] = z_row[:, 0:TILE]
+
+    @pl.when(r == 1)
+    def _():
+        white[0:1, :] = z_row[:, TILE:PANEL]
+
+    write_rows.wait()
+    for copy in writes:
+        copy.wait()
 
 
 def per_device(covariance, observations):
     obs = observations.reshape(16, TILE)
     dma = pltpu.SemaphoreType.DMA
-    hbm = pl.BlockSpec(memory_space=pl.ANY)
+    any_space = pl.BlockSpec(memory_space=pl.ANY)
+    hbm = pl.BlockSpec(memory_space=pltpu.HBM)
     vmem = pl.BlockSpec(memory_space=pltpu.VMEM)
-    pan, cols, heads, lead, inv = pl.pallas_call(
+    pan, cols, heads, inv, cov_here, obs_here = pl.pallas_call(
         gather_kernel,
         out_shape=[
             jax.ShapeDtypeStruct((4, NX, 2, CHUNK, PANEL), F32),
             jax.ShapeDtypeStruct((2, TILE, 512), F32),
             jax.ShapeDtypeStruct((2, 8, TILE), F32),
             jax.ShapeDtypeStruct((PANEL, PANEL), F32),
-            jax.ShapeDtypeStruct((PANEL, PANEL), F32),
+            jax.ShapeDtypeStruct((2048, 512), F32),
+            jax.ShapeDtypeStruct((16, TILE), F32),
         ],
         in_specs=[hbm, hbm],
-        out_specs=[hbm, hbm, hbm, vmem, vmem],
+        out_specs=[any_space, any_space, any_space, vmem, any_space, any_space],
         scratch_shapes=[
             pltpu.VMEM((NZ, 3, SLICE, TILE), F32),
             pltpu.VMEM((4, TILE, TILE), F32),
             pltpu.VMEM((TILE, PANEL), F32),
             pltpu.VMEM((TILE, 512), F32),
-            dma((1,)),
+            dma((3,)),
             dma((8,)), dma((3,)), dma((16,)), dma, dma((8,)), dma((8,)), dma, dma,
-            dma((8,)), dma((2,)), dma((8,)), dma((8,)), dma((4,)), dma((4,)),
-            dma((4, 8)), dma((4, 8)), dma((8, 4)), dma((4, 8)),
+            dma((8,)), dma((2,)), dma((4,)), dma((4,)),
+            dma((4, 5)), dma((4, 5)), dma((4, 5)), dma((4, 5)), dma((8, 4)), dma((8, 4)),
             dma((4,)), dma((2,)), dma((4,)), dma((2,)),
         ],
-        compiler_params=pltpu.CompilerParams(collective_id=0, has_side_effects=True, vmem_limit_bytes=32 << 20),
+        compiler_params=pltpu.CompilerParams(collective_id=0, has_side_effects=True, vmem_limit_bytes=46 << 20),
     )(covariance, obs)
-    rows = 256
-    fixed = lambda *shape: pl.BlockSpec(shape, lambda i: (0,) * len(shape))
     out, fac, white = pl.pallas_call(
         update_kernel,
-        grid=(2048 // rows,),
         out_shape=[
             jax.ShapeDtypeStruct((2048, 512), F32),
             jax.ShapeDtypeStruct((2048, PANEL), F32),
             jax.ShapeDtypeStruct((16, TILE), F32),
         ],
-        in_specs=[
-            pl.BlockSpec((rows, 512), lambda i: (i, 0)),
-            pl.BlockSpec((rows, PANEL), lambda i: (i, 0)),
-            fixed(16, TILE),
-            fixed(PANEL, 512),
-            fixed(2, 8, TILE),
-            fixed(PANEL, PANEL),
-            fixed(PANEL, PANEL),
+        in_specs=[vmem] * 6,
+        out_specs=[any_space, any_space, vmem],
+        scratch_shapes=[
+            pltpu.VMEM((2048, PANEL), F32),
+            pltpu.VMEM((2048, 512), F32),
+            dma((1 + PARTS,)),
         ],
-        out_specs=[
-            pl.BlockSpec((rows, 512), lambda i: (i, 0)),
-            pl.BlockSpec((rows, PANEL), lambda i: (i, 0)),
-            fixed(16, TILE),
-        ],
-        scratch_shapes=[
-            pltpu.VMEM((3, PANEL, PANEL), BF16),
-            pltpu.VMEM((PANEL, 512), BF16),
-            pltpu.VMEM((PANEL, 512), BF16),
-            pltpu.VMEM((8, PANEL), F32),
-        ],
-        compiler_params=pltpu.CompilerParams(vmem_limit_bytes=32 << 20),
-    )(covariance, pan.reshape(2048, PANEL), obs, cols.reshape(PANEL, 512), heads, lead, inv)
+        compiler_params=pltpu.CompilerParams(vmem_limit_bytes=36 << 20),
+    )(cov_here, pan.reshape(2048, PANEL), obs_here, cols.reshape(PANEL, 512), heads, inv)
     return out, fac, white.reshape(2048)
 
 

time: 70.1 us -> 58.9 us (0.84)
  Pallas kernels: 66.4 us -> 56.8 us
  local copies, waits for them, and re-layouts: 2.88 us -> 0.69 us
    pallas_call x1, Pallas kernels: 56.4 us -> 47.7 us  [per_device(): pl.pallas_call(gather_kernel, out_shape=[jax.ShapeDtypeStruct((4, NX, 2,...]
    unnamed x4 -> x2, local copies, waits for them, and re-layouts: 2.88 us -> 0.69 us
    pallas_call x1, Pallas kernels: 10 us -> 9.08 us  [per_device(): pl.pallas_call(update_kernel, out_shape=[jax.ShapeDtypeStruct((2048, 512)...]
where the time goes in v2:
time: 58.9 us; the launch traced here: 58.1 us
  Pallas kernels  56.8 us (96%)
  local copies, waits for them, and re-layouts  0.69 us (1%)
  between operations  0.65 us (1%)
    pallas_call x1, Pallas kernels, per_device(): pl.pallas_call(gather_kernel, out_shape=[jax.ShapeDtypeStruct((4, NX, 2,...  47.7 us
    pallas_call x1, Pallas kernels, per_device(): pl.pallas_call(update_kernel, out_shape=[jax.ShapeDtypeStruct((2048, 512)...  9.08 us

profile of v2, /device:TPU:16, one launch (start us, length us, event | category | flops | bytes accessed | tf_op | source)
XLA Modules:
  0.0 58.1 jit_solution(7662276288012979509)
XLA Ops:
  0.6 0.0 copy-start
  0.6 0.7 %copy-done = f32[2048]{0:T(1024)S(1)} copy-done((f32[2048]{0:T(1024)S(1)}, f32[2048]{0:T(1024)}, u32[]{:S(2)}) %copy-start) | copy-done | bytes 8216
  1.3 47.7 %shard_map.49 = (f32[4,4,2,64,256]{4,3,2,1,0:T(8,128)S(1)}, f32[2,128,512]{2,1,0:T(8,128)S(1)}, f32[2,8,128]{2,1,0:T(8,128)S(1)}, f32[256,256]{1,0:T(8,128)S(1)}...) custom-call(f32[2048,512]{1,0:T(8,128)} %cov.1, f32[16,128]{1,0:T(8,128)S(1)} %bitcast.6), custom_call_target="tpu_custom_call" | custom-call | tf_op jit(solution)/shard_map/pallas_call | solution.py:505
  49.1 9.1 %shard_map.50 = (f32[2048,512]{1,0:T(8,128)}, f32[2048,256]{1,0:T(8,128)}, f32[16,128]{1,0:T(8,128)}) custom-call(f32[2048,512]{1,0:T(8,128)S(1)} %get-tuple-element.12.cov, f32[2048,256]{1,0:T(8,128)S(1)} %bitcast.4, f32[16,128]{1,0:T(8,128)S(1)} %get-tuple-element.14.obs, f32[256,512]{1,0:T(8,128)S(1)} %bitcast.5, ...), custom_call_target="tpu_custom_call" | custom-call | tf_op jit(solution)/shard_map/pallas_call | solution.py:530
Async XLA Ops:
  0.6 0.7 %copy-start = (f32[2048]{0:T(1024)S(1)}, f32[2048]{0:T(1024)}, u32[]{:S(2)}) copy-start(f32[2048]{0:T(1024)} %param.3) | copy-start | bytes 24580

commit v3 on v2

--- a/solution.py
+++ b/solution.py
@@ -102,9 +102,9 @@
 
 
 def gather_kernel(
-    cov, obs, pan, cols, heads, inv_out, cov_here, obs_here,
-    lead, turn, work, saved,
-    load_sem, l1_send, l1_recv, l2_send, l2_recv, l3_send, l3_recv, sib_send, sib_recv,
+    cov, obs, fac_here, cov_here, col_high, col_low, white,
+    pan, cols, heads, obs_here, rows, inv, acc, lead, turn, work, saved,
+    load_sem, out_sem, l1_send, l1_recv, l2_send, l2_recv, l3_send, l3_recv, sib_send, sib_recv,
     sc_send, sc_recv, x_send, x_recv, up_send, up_recv, down_send, down_recv, side_send, side_recv,
     c_send, c_recv, h_send, h_recv,
 ):
@@ -190,6 +190,28 @@
     def mine(kk):
         return lead.at[z, 0:1] if kk == 0 else lead.at[z, 1:3]
 
+    @pl.when(at_source)
+    def _():
+        for kk in range(2):
+
+            @pl.when(r == kk)
+            def _():
+                for i in (4, 3, 5, 2, 6, 1, 7, 0):
+                    zz = (z + i) % NZ
+                    src = turn.at[zz // 2, pl.ds(pl.multiple_of(CHUNK * (zz % 2), CHUNK), CHUNK), :]
+                    dst = pan.at[zz // 2, x, zz % 2, :, kk * TILE : (kk + 1) * TILE]
+                    if i:
+                        remote(src, dst, sc_send.at[i], sc_recv.at[kk], z, x * NZ + zz).start()
+                    else:
+
+                        @pl.when(z == kk)
+                        def _():
+                            pltpu.make_async_copy(src, dst, sc_recv.at[kk]).start()
+
+                        @pl.when(z != kk)
+                        def _():
+                            remote(src, dst, sc_send.at[i], sc_recv.at[kk], z, x * NZ + zz).start()
+
     for kk in range(2):
 
         @pl.when((r == kk) & in_root_plane)
@@ -218,24 +240,6 @@
             for i in range(1, NZ):
                 remote(mine(kk), mine(kk), l3_send.at[i], l3_recv.at[z], r, z_peer(i)).start()
 
-    @pl.when(at_source)
-    def _():
-        for kk in range(2):
-
-            @pl.when(r == kk)
-            def _():
-                for i in range(NZ):
-                    src = turn.at[i // 2, CHUNK * (i % 2) : CHUNK * (i % 2 + 1), :]
-                    dst = pan.at[i // 2, x, i % 2, :, kk * TILE : (kk + 1) * TILE]
-
-                    @pl.when((z == kk) & (z == i))
-                    def _():
-                        pltpu.make_async_copy(src, dst, sc_recv.at[kk]).start()
-
-                    @pl.when(jnp.logical_not((z == kk) & (z == i)))
-                    def _():
-                        remote(src, dst, sc_send.at[i], sc_recv.at[kk], z, x * NZ + i).start()
-
     own = pan.at[z // 2, x, z % 2]
     for kk in range(2):
         wait_bytes(pan.at[z // 2, x, z % 2, :, kk * TILE : (kk + 1) * TILE], sc_recv.at[kk])
@@ -355,8 +359,8 @@
 
     lax.fori_loop(0, TILE // NB, first, 0)
     inv_one = triangle(work[:, TILE:], True)
-    inv_out[0:TILE, 0:TILE] = inv_one
-    inv_out[0:TILE, TILE:PANEL] = jnp.zeros((TILE, TILE), F32)
+    inv[0:TILE, 0:TILE] = inv_one
+    inv[0:TILE, TILE:PANEL] = jnp.zeros((TILE, TILE), F32)
     below = mul6(block(1), inv_one, NT)
     init_work(work, block(2) - mul6(below, below, NT))
     joint = mul6(below, inv_one, NN)
@@ -382,8 +386,8 @@
 
     lax.fori_loop(0, TILE // NB, second, 0)
     inv_two = triangle(work[:, TILE:], True)
-    inv_out[TILE:PANEL, TILE:PANEL] = inv_two
-    inv_out[TILE:PANEL, 0:TILE] = -mul6(inv_two, joint, NN)
+    inv[TILE:PANEL, TILE:PANEL] = inv_two
+    inv[TILE:PANEL, 0:TILE] = -mul6(inv_two, joint, NN)
 
     for kk in range(2):
 
@@ -392,14 +396,63 @@
             wait_bytes(cols.at[kk], c_recv.at[1])
             wait_bytes(heads.at[kk], h_recv.at[1])
 
-    other_columns(NZ // 2)
-    for i in range(1, NX):
-        xx = (x + i) % NX
-        for j in range(1, NZ):
-            zz = (z + j) % NZ
-            wait_bytes(chunk(xx, zz, HALF, HALF), side_recv.at[zz, xx])
+    first_obs = jnp.concatenate([heads[0, 0:1, :], heads[1, 0:1, :]], 1)
+    z_row = mul6(jnp.broadcast_to(first_obs, (8, PANEL)), inv[...], NT)[0:1, :]
+    col_high[...], col_low[...] = split2(mul6(inv[...], cols[...].reshape(PANEL, 512), NN))
+    i_h, i_m, i_l = split3(inv[...].T)
+    lane = lax.broadcasted_iota(jnp.int32, (CHUNK, TILE), 1)
+    r_at = lax.broadcasted_iota(jnp.int32, (CHUNK, PANEL), 0)
+    c_at = lax.broadcasted_iota(jnp.int32, (CHUNK, PANEL), 1)
+
+    def factor_block(n, _):
+        off = jnp.where(n % 2 == 1, (n + 1) // 2, (NZ - n // 2) % NZ)
+        zz = (z + off) % NZ
+        s, h = zz // 2, zz % 2
+
+        @pl.when(n == NZ - 1)
+        def _():
+            other_columns(NZ // 2)
+
+        @pl.when(n > 0)
+        def _():
+            for i in range(1, NX):
+                xx = (x + i) % NX
+                wait_bytes(chunk(xx, zz, HALF, HALF), side_recv.at[zz, xx])
+
+        p_h, p_m, p_l = split3(pan[s, :, h].reshape(PANEL, PANEL))
+        small = mul(p_h, i_l, NN) + mul(p_l, i_h, NN) + mul(p_m, i_m, NN)
+        part = small + (mul(p_h, i_m, NN) + mul(p_m, i_h, NN)) + mul(p_h, i_h, NN)
+        rows[s, :, h] = part.reshape(NX, CHUNK, PANEL)
+
+        @pl.when((r < 2) & (zz < 2))
+        def _():
+            rows[0, 0, h] = jnp.where(c_at <= r_at + CHUNK * h + TILE * r, rows[0, 0, h], 0.0)
+
+        pltpu.make_async_copy(rows.at[s, :, h], fac_here.at[s, :, h], out_sem.at[n]).start()
+        here = pl.ds(pl.multiple_of(CHUNK * h, CHUNK), CHUNK)
+        sums = acc[here, :]
+        for xx in range(NX):
+            dots = jnp.sum(part[xx * CHUNK : (xx + 1) * CHUNK] * z_row, axis=1, keepdims=True)
+            sums = jnp.where(lane == NX * s + xx, dots, sums)
+        acc[here, :] = sums
+        return 0
+
+    acc[...] = jnp.zeros((TILE, TILE), F32)
+    lax.fori_loop(0, NZ, factor_block, 0)
+    load_obs.wait()
+    white[...] = obs_here[...] - acc[...].T[0:16]
+
+    @pl.when(r == 0)
+    def _():
+        white[0:1, :] = z_row[:, 0:TILE]
+
+    @pl.when(r == 1)
+    def _():
+        white[0:1, :] = z_row[:, TILE:PANEL]
+
     load_cov.wait()
-    load_obs.wait()
+    for n in range(NZ):
+        wait_bytes(rows.at[0, :, 0], out_sem.at[n])
 
     for i in range(NX):
         rows = CHUNK if i == 0 else HALF
@@ -426,11 +479,12 @@
             for i in range(1, 4):
                 wait_bytes(cols.at[kk], c_send.at[i])
                 wait_bytes(heads.at[kk], h_send.at[i])
-            for i in range(NZ):
-
-                @pl.when(jnp.logical_not((z == kk) & (z == i)))
-                def _():
-                    wait_bytes(turn.at[0, 0:CHUNK, :], sc_send.at[i])
+            for i in range(1, NZ):
+                wait_bytes(turn.at[0, 0:CHUNK, :], sc_send.at[i])
+
+            @pl.when(z != kk)
+            def _():
+                wait_bytes(turn.at[0, 0:CHUNK, :], sc_send.at[0])
 
         @pl.when((r == kk) & in_root_plane)
         def _():
@@ -446,27 +500,10 @@
                 wait_bytes(lead.at[0, 0], l1_send.at[i])
 
 
-def update_kernel(cov, pan, obs, cols, heads, inv, out, fac, white, rows, done, sems):
-    r = lax.axis_index("row")
-    h, m, l = split3(inv[...].T)
-    p_h, p_m, p_l = split3(pan[...])
-    small = mul(p_h, l, NN) + mul(p_l, h, NN) + mul(p_m, m, NN)
-    rows[...] = small + (mul(p_h, m, NN) + mul(p_m, h, NN)) + mul(p_h, h, NN)
-
-    @pl.when(r == 0)
-    def _():
-        rows[0:TILE, 0:TILE] = triangle(rows[0:TILE, 0:TILE], True)
-        rows[0:TILE, TILE:PANEL] = jnp.zeros((TILE, TILE), F32)
-
-    @pl.when(r == 1)
-    def _():
-        rows[0:TILE, TILE:PANEL] = triangle(rows[0:TILE, TILE:PANEL], True)
-
+def update_kernel(cov, rows, col_high, col_low, white_in, out, fac, white, done, sems):
     write_rows = pltpu.make_async_copy(rows, fac, sems.at[0])
     write_rows.start()
-    c_h, c_l = split2(mul6(inv[...], cols[...], NN))
-    first = jnp.concatenate([heads[0, 0:1, :], heads[1, 0:1, :]], 1)
-    z_row = mul6(jnp.broadcast_to(first, (8, PANEL)), inv[...], NT)[0:1, :]
+    c_h, c_l = col_high[...], col_low[...]
     writes = []
     for i in range(PARTS):
         n = 2048 // PARTS
@@ -476,21 +513,7 @@
         copy = pltpu.make_async_copy(done.at[at, :], out.at[at, :], sems.at[1 + i])
         copy.start()
         writes.append(copy)
-    lane = lax.broadcasted_iota(jnp.int32, (TILE, TILE), 1)
-    acc = jnp.zeros((TILE, TILE), F32)
-    for t in range(16):
-        part = jnp.sum(rows[t * TILE : (t + 1) * TILE, :] * z_row, axis=1, keepdims=True)
-        acc = jnp.where(lane == t, part, acc)
-    white[...] = obs[...] - acc.T[0:16]
-
-    @pl.when(r == 0)
-    def _():
-        white[0:1, :] = z_row[:, 0:TILE]
-
-    @pl.when(r == 1)
-    def _():
-        white[0:1, :] = z_row[:, TILE:PANEL]
-
+    white[...] = white_in[...]
     write_rows.wait()
     for copy in writes:
         copy.wait()
@@ -500,26 +523,31 @@
     obs = observations.reshape(16, TILE)
     dma = pltpu.SemaphoreType.DMA
     any_space = pl.BlockSpec(memory_space=pl.ANY)
-    hbm = pl.BlockSpec(memory_space=pltpu.HBM)
     vmem = pl.BlockSpec(memory_space=pltpu.VMEM)
-    pan, cols, heads, inv, cov_here, obs_here = pl.pallas_call(
+    fac_here, cov_here, col_high, col_low, white = pl.pallas_call(
         gather_kernel,
         out_shape=[
             jax.ShapeDtypeStruct((4, NX, 2, CHUNK, PANEL), F32),
-            jax.ShapeDtypeStruct((2, TILE, 512), F32),
-            jax.ShapeDtypeStruct((2, 8, TILE), F32),
-            jax.ShapeDtypeStruct((PANEL, PANEL), F32),
             jax.ShapeDtypeStruct((2048, 512), F32),
+            jax.ShapeDtypeStruct((PANEL, 512), BF16),
+            jax.ShapeDtypeStruct((PANEL, 512), BF16),
             jax.ShapeDtypeStruct((16, TILE), F32),
         ],
-        in_specs=[hbm, hbm],
-        out_specs=[any_space, any_space, any_space, vmem, any_space, any_space],
+        in_specs=[any_space, any_space],
+        out_specs=[any_space, any_space, vmem, vmem, vmem],
         scratch_shapes=[
+            pltpu.VMEM((4, NX, 2, CHUNK, PANEL), F32),
+            pltpu.VMEM((2, TILE, 512), F32),
+            pltpu.VMEM((2, 8, TILE), F32),
+            pltpu.VMEM((16, TILE), F32),
+            pltpu.VMEM((4, NX, 2, CHUNK, PANEL), F32),
+            pltpu.VMEM((PANEL, PANEL), F32),
+            pltpu.VMEM((TILE, TILE), F32),
             pltpu.VMEM((NZ, 3, SLICE, TILE), F32),
             pltpu.VMEM((4, TILE, TILE), F32),
             pltpu.VMEM((TILE, PANEL), F32),
             pltpu.VMEM((TILE, 512), F32),
-            dma((3,)),
+            dma((3,)), dma((NZ,)),
             dma((8,)), dma((3,)), dma((16,)), dma, dma((8,)), dma((8,)), dma, dma,
             dma((8,)), dma((2,)), dma((4,)), dma((4,)),
             dma((4, 5)), dma((4, 5)), dma((4, 5)), dma((4, 5)), dma((8, 4)), dma((8, 4)),
@@ -534,15 +562,14 @@
             jax.ShapeDtypeStruct((2048, PANEL), F32),
             jax.ShapeDtypeStruct((16, TILE), F32),
         ],
-        in_specs=[vmem] * 6,
+        in_specs=[vmem] * 5,
         out_specs=[any_space, any_space, vmem],
         scratch_shapes=[
-            pltpu.VMEM((2048, PANEL), F32),
             pltpu.VMEM((2048, 512), F32),
             dma((1 + PARTS,)),
         ],
         compiler_params=pltpu.CompilerParams(vmem_limit_bytes=36 << 20),
-    )(cov_here, pan.reshape(2048, PANEL), obs_here, cols.reshape(PANEL, 512), heads, inv)
+    )(cov_here, fac_here.reshape(2048, PANEL), col_high, col_low, white)
     return out, fac, white.reshape(2048)
 
 

time: 58.9 us -> 52.5 us (0.89)
  Pallas kernels: 56.8 us -> 50.4 us
    pallas_call x1, Pallas kernels: 9.08 us -> 3.42 us  [per_device(): pl.pallas_call(update_kernel, out_shape=[jax.ShapeDtypeStruct((2048, 512)...]
    pallas_call x1, Pallas kernels: 47.7 us -> 47 us  [per_device(): pl.pallas_call(gather_kernel, out_shape=[jax.ShapeDtypeStruct((4, NX, 2,...]
where the time goes in v3:
time: 52.5 us; the launch traced here: 51.8 us
  Pallas kernels  50.4 us (96%)
  local copies, waits for them, and re-layouts  0.69 us (1%)
  between operations  0.65 us (1%)
    pallas_call x1, Pallas kernels, per_device(): pl.pallas_call(gather_kernel, out_shape=[jax.ShapeDtypeStruct((4, NX, 2,...  47 us
    pallas_call x1, Pallas kernels, per_device(): pl.pallas_call(update_kernel, out_shape=[jax.ShapeDtypeStruct((2048, 512)...  3.42 us

profile of v3, /device:TPU:16, one launch (start us, length us, event | category | flops | bytes accessed | tf_op | source)
XLA Modules:
  0.0 51.8 jit_solution(12876280076313368474)
XLA Ops:
  0.6 0.0 copy-start
  0.6 0.7 %copy-done = f32[2048]{0:T(1024)S(1)} copy-done((f32[2048]{0:T(1024)S(1)}, f32[2048]{0:T(1024)}, u32[]{:S(2)}) %copy-start) | copy-done | bytes 8216
  1.3 47.0 %shard_map.49 = (f32[4,4,2,64,256]{4,3,2,1,0:T(8,128)S(1)}, f32[2048,512]{1,0:T(8,128)S(1)}, bf16[256,512]{1,0:T(8,128)(2,1)S(1)}, bf16[256,512]{1,0:T(8,128)(2,1)S(1)}, f32[16,128]{1,0:T(8,128)S(1)}) custom-call(f32[2048,512]{1,0:T(8,128)} %cov.1, f32[16,128]{1,0:T(8,128)S(1)} %bitcast.4), custom_call_target="tpu_custom_call" | custom-call | tf_op jit(solution)/shard_map/pallas_call | solution.py:527
  48.3 3.4 %shard_map.50 = (f32[2048,512]{1,0:T(8,128)}, f32[2048,256]{1,0:T(8,128)}, f32[16,128]{1,0:T(8,128)}) custom-call(f32[2048,512]{1,0:T(8,128)S(1)} %get-tuple-element.11.cov, f32[2048,256]{1,0:T(8,128)S(1)} %bitcast.3, bf16[256,512]{1,0:T(8,128)(2,1)S(1)} %get-tuple-element.13.col_high, bf16[256,512]{1,0:T(8,128)(2,1)S(1)} %get-tuple-element.14.col_low, ...), custom_call_target="tpu_custom_call" | custom-call | tf_op jit(solution)/shard_map/pallas_call | solution.py:558
Async XLA Ops:
  0.6 0.7 %copy-start = (f32[2048]{0:T(1024)S(1)}, f32[2048]{0:T(1024)}, u32[]{:S(2)}) copy-start(f32[2048]{0:T(1024)} %param.3) | copy-start | bytes 24580

commit v4 on v3

--- a/solution.py
+++ b/solution.py
@@ -14,6 +14,7 @@
 HALF = CHUNK // 2
 QUARTER = CHUNK // 4
 PARTS = 4
+OWN = NX
 SLICE = TILE // NZ
 F32, BF16 = jnp.float32, jnp.bfloat16
 
@@ -62,34 +63,48 @@
     here = pl.ds(pl.multiple_of(base, NB), NB)
     rows = work[here, :]
     turned = pltpu.roll(rows[:, :TILE], lax.rem(TILE - base, TILE), 1)
-    cols = [jnp.broadcast_to(turned[:, j : j + 1], (NB, TILE)) for j in range(NB)]
-    el = [[jnp.broadcast_to(cols[j][i : i + 1, :], (8, TILE)) for j in range(i + 1)] for i in range(NB)]
-    left = [jnp.broadcast_to(rows[i : i + 1, :TILE], (8, TILE)) for i in range(NB)]
-    right = [jnp.broadcast_to(rows[i : i + 1, TILE:], (8, TILE)) for i in range(NB)]
-    for j in range(NB):
-        inv = lax.rsqrt(el[j][j])
-        left[j] = left[j] * inv
-        right[j] = right[j] * inv
-        low = [None] * NB
-        for i in range(j + 1, NB):
-            low[i] = el[i][j] * inv
-        for i in range(j + 1, NB):
-            for k in range(j + 1, i + 1):
-                el[i][k] = el[i][k] - low[i] * low[k]
-            left[i] = left[i] - low[i] * left[j]
-            right[i] = right[i] - low[i] * right[j]
     sub = lax.broadcasted_iota(jnp.int32, (8, TILE), 0)
 
-    def pack(parts):
-        halves = []
-        for h in range(NB // 8):
-            acc = parts[h * 8]
-            for i in range(1, 8):
-                acc = jnp.where(sub == i, parts[h * 8 + i], acc)
-            halves.append(acc)
-        return jnp.concatenate(halves, 0)
-
-    u_left, u_right = pack(left), pack(right)
+    def column(top, j):
+        return jnp.broadcast_to(turned[top : top + 8, j : j + 1], (8, TILE))
+
+    def spread(x, i):
+        return jnp.broadcast_to(x[i : i + 1, :], (8, TILE))
+
+    def factor(diag, others, sides):
+        el = [[spread(diag[j], i) for j in range(i + 1)] for i in range(8)]
+        top = sides[0]
+        for j in range(8):
+            inv = lax.rsqrt(el[j][j])
+            low = [None] * 8
+            for i in range(j + 1, 8):
+                low[i] = el[i][j] * inv
+            for i in range(j + 1, 8):
+                for k in range(j + 1, i + 1):
+                    el[i][k] = el[i][k] - low[i] * low[k]
+            for cols in [diag] + others:
+                cols[j] = cols[j] * inv
+                for k in range(j + 1, 8):
+                    cols[k] = cols[k] - cols[j] * low[k]
+            below = jnp.where(sub > j, diag[j], 0.0)
+            for n in range(2):
+                row = spread(top[n], j) * inv
+                top[n] = jnp.where(sub == j, row, top[n] - below * row)
+                for cols, side in zip(others, sides[1:]):
+                    side[n] = side[n] - cols[j] * row
+
+    a11 = [column(0, j) for j in range(8)]
+    a21 = [column(8, j) for j in range(8)]
+    a22 = [column(8, 8 + j) for j in range(8)]
+    r1 = [rows[0:8, :TILE], rows[0:8, TILE:]]
+    r2 = [rows[8:16, :TILE], rows[8:16, TILE:]]
+    factor(a11, [a21], [r1, r2])
+    for k in range(8):
+        for j in range(8):
+            a22[k] = a22[k] - a21[j] * spread(a21[j], k)
+    factor(a22, [], [r2])
+    u_left = jnp.concatenate([r1[0], r2[0]], 0)
+    u_right = jnp.concatenate([r1[1], r2[1]], 0)
     lane = lax.broadcasted_iota(jnp.int32, (NB, TILE), 1)
     below = jnp.where(lane >= base + NB, u_left, 0.0)
     u = jnp.concatenate([u_left, u_right], 1)
@@ -190,27 +205,34 @@
     def mine(kk):
         return lead.at[z, 0:1] if kk == 0 else lead.at[z, 1:3]
 
+    def chunk(xx, zz, first, count, half=None):
+        if half is None:
+            return pan.at[zz // 2, xx, zz % 2, first : first + count, :]
+        return pan.at[zz // 2, xx, zz % 2, first : first + count, half * TILE : (half + 1) * TILE]
+
     @pl.when(at_source)
     def _():
         for kk in range(2):
 
             @pl.when(r == kk)
             def _():
-                for i in (4, 3, 5, 2, 6, 1, 7, 0):
-                    zz = (z + i) % NZ
-                    src = turn.at[zz // 2, pl.ds(pl.multiple_of(CHUNK * (zz % 2), CHUNK), CHUNK), :]
-                    dst = pan.at[zz // 2, x, zz % 2, :, kk * TILE : (kk + 1) * TILE]
-                    if i:
-                        remote(src, dst, sc_send.at[i], sc_recv.at[kk], z, x * NZ + zz).start()
-                    else:
-
-                        @pl.when(z == kk)
-                        def _():
-                            pltpu.make_async_copy(src, dst, sc_recv.at[kk]).start()
-
-                        @pl.when(z != kk)
-                        def _():
-                            remote(src, dst, sc_send.at[i], sc_recv.at[kk], z, x * NZ + zz).start()
+                for part in range(2):
+                    for i in (4, 3, 5, 2, 6, 1, 7, 0):
+                        zz = (z + i) % NZ
+                        low = pl.multiple_of(CHUNK * (zz % 2) + HALF * part, HALF)
+                        src = turn.at[zz // 2, pl.ds(low, HALF), :]
+                        dst = chunk(x, zz, HALF * part, HALF, kk)
+                        if i:
+                            remote(src, dst, sc_send.at[part, i], sc_recv.at[kk, part], z, x * NZ + zz).start()
+                        else:
+
+                            @pl.when(z == kk)
+                            def _():
+                                pltpu.make_async_copy(src, dst, sc_recv.at[kk, part]).start()
+
+                            @pl.when(z != kk)
+                            def _():
+                                remote(src, dst, sc_send.at[part, i], sc_recv.at[kk, part], z, x * NZ + zz).start()
 
     for kk in range(2):
 
@@ -221,8 +243,8 @@
             else:
                 wait_bytes(lead.at[z, 1], l1_recv.at[1])
                 wait_bytes(lead.at[z, 2], l1_recv.at[2])
-            for yy in range(4):
-                for xx in range(NX):
+            for yy in (2, 1, 3, 0):
+                for xx in (2, 1, 3, 0):
                     if (yy, xx) != (0, 0):
                         remote(
                             mine(kk), mine(kk), l2_send.at[yy * NX + xx], l2_recv, 2 * yy + kk, xx * NZ + z
@@ -237,60 +259,56 @@
             def _():
                 wait_bytes(mine(kk), l2_recv)
 
-            for i in range(1, NZ):
+            for i in (4, 3, 5, 2, 6, 1, 7):
                 remote(mine(kk), mine(kk), l3_send.at[i], l3_recv.at[z], r, z_peer(i)).start()
 
-    own = pan.at[z // 2, x, z % 2]
-    for kk in range(2):
-        wait_bytes(pan.at[z // 2, x, z % 2, :, kk * TILE : (kk + 1) * TILE], sc_recv.at[kk])
-
-    def chunk(xx, zz, first, count):
-        return pan.at[zz // 2, xx, zz % 2, first : first + count, :]
-
-    def pass_on(i, d, first, count):
-        xx = (x + i) % NX
-        for way, send, recv in ((1, up_send, up_recv), (-1, down_send, down_recv)):
-            zz = (z - way * (d - 1) + NZ) % NZ
-            low, rows = first, count
-            if d == NZ // 2:
-                rows = count // 2
-                low = first if way == 1 else first + rows
-            part = chunk(xx, zz, low, rows)
-            remote(part, part, send.at[i, d], recv.at[i, d], r, x * NZ + (z + way + NZ) % NZ).start()
-
-    def landed(i, d, first, count):
-        xx = (x + i) % NX
+    def stream(i):
+        return ((x + i) % NX, 0) if i < OWN else (x, HALF)
+
+    def piece(i, zz, d, way):
+        xx, first = stream(i)
+        if d < NZ // 2:
+            return chunk(xx, zz, first, HALF)
+        return chunk(xx, zz, first if way == 1 else first + QUARTER, QUARTER)
+
+    def push(i, d, way):
+        send, recv = (up_send, up_recv) if way == 1 else (down_send, down_recv)
+        part = piece(i, (z - way * (d - 1) + NZ) % NZ, d, way)
+        remote(part, part, send.at[i, d], recv.at[i, d], r, x * NZ + (z + way + NZ) % NZ).start()
+
+    def hop(i, d):
         for way, recv in ((1, up_recv), (-1, down_recv)):
-            zz = (z - way * d + NZ) % NZ
-            low, rows = first, count
-            if d == NZ // 2:
-                rows = count // 2
-                low = first if way == 1 else first + rows
-            wait_bytes(chunk(xx, zz, low, rows), recv.at[i, d])
-
-    def sideways(zz, d, way):
+            wait_bytes(piece(i, (z - way * d + NZ) % NZ, d, way), recv.at[i, d])
+            if d < NZ // 2:
+                push(i, d + 1, way)
+
+    def sideways(zz, slot):
         part = chunk(x, zz, HALF, HALF)
-        for j in range(1, NX):
-            remote(part, part, side_send.at[d, j], side_recv.at[zz, x], r, x_peer(j)).start()
+        for j in (2, 1, 3):
+            remote(part, part, side_send.at[slot, j], side_recv.at[zz, x], r, x_peer(j)).start()
 
     def own_column(d):
-        landed(0, d, 0, CHUNK)
+        hop(OWN, d)
+        sideways((z - d + NZ) % NZ, d)
         if d < NZ // 2:
-            pass_on(0, d + 1, 0, CHUNK)
-            sideways((z - d + NZ) % NZ, d, 1)
-            sideways((z + d) % NZ, NZ - d, -1)
-        else:
-            sideways((z + d) % NZ, d, -1)
+            sideways((z + d) % NZ, NZ - d)
 
     def other_columns(d):
-        for i in range(1, NX):
-            landed(i, d, 0, HALF)
-            if d < NZ // 2:
-                pass_on(i, d + 1, 0, HALF)
-
-    pass_on(0, 1, 0, CHUNK)
-    for i in range(1, NX):
-        remote(own, own, x_send.at[i], x_recv.at[x], r, x_peer(i)).start()
+        for i in (1, 3, 2):
+            hop(i, d)
+
+    for kk in range(2):
+        wait_bytes(chunk(x, z, 0, HALF, kk), sc_recv.at[kk, 0])
+    for i in (2, 1, 3):
+        part = chunk(x, z, 0, HALF)
+        remote(part, part, x_send.at[i], x_recv.at[x], r, x_peer(i)).start()
+    for way in (1, -1):
+        push(0, 1, way)
+    for kk in range(2):
+        wait_bytes(chunk(x, z, HALF, HALF, kk), sc_recv.at[kk, 1])
+    for way in (1, -1):
+        push(OWN, 1, way)
+    sideways(z, 0)
 
     for kk in range(2):
 
@@ -308,12 +326,6 @@
     load_obs = pltpu.make_async_copy(obs, obs_here, load_sem.at[2])
     load_obs.start()
 
-    own_column(1)
-    for i in range(1, NX):
-        xx = (x + i) % NX
-        wait_bytes(chunk(xx, z, 0, CHUNK), x_recv.at[xx])
-        pass_on(i, 1, 0, HALF)
-
     def gathered(kk, zz):
         return lead.at[zz, 0:1] if kk == 0 else lead.at[zz, 1:3]
 
@@ -329,6 +341,13 @@
                 wait_bytes(gathered(kk, zz), l3_recv.at[zz])
             remote(whole(kk), whole(kk), sib_send, sib_recv, sib, c).start()
 
+    own_column(1)
+    hop(0, 1)
+    for i in (1, 3, 2):
+        wait_bytes(chunk((x + i) % NX, z, 0, HALF), x_recv.at[(x + i) % NX])
+        for way in (1, -1):
+            push(i, 1, way)
+
     for kk in range(2):
 
         @pl.when(k != kk)
@@ -338,13 +357,8 @@
     def block(b):
         return lead[:, b].reshape(TILE, TILE)
 
-    FIRST = (
-        (1, lambda: own_column(2)),
-        (2, lambda: other_columns(1)),
-        (4, lambda: own_column(3)),
-        (6, lambda: other_columns(2)),
-    )
-    SECOND = ((0, lambda: own_column(4)), (2, lambda: other_columns(3)))
+    FIRST = ((3, lambda: own_column(2)), (4, lambda: hop(0, 2)), (6, lambda: other_columns(1)), )
+    SECOND = ((0, lambda: own_column(3)), (1, lambda: hop(0, 3)), (2, lambda: other_columns(2)), (5, lambda: own_column(4)), (7, lambda: other_columns(3)), )
     init_work(work, block(0))
 
     def first(g, _):
@@ -411,13 +425,12 @@
 
         @pl.when(n == NZ - 1)
         def _():
+            hop(0, NZ // 2)
             other_columns(NZ // 2)
 
-        @pl.when(n > 0)
-        def _():
-            for i in range(1, NX):
-                xx = (x + i) % NX
-                wait_bytes(chunk(xx, zz, HALF, HALF), side_recv.at[zz, xx])
+        for i in range(1, NX):
+            xx = (x + i) % NX
+            wait_bytes(chunk(xx, zz, HALF, HALF), side_recv.at[zz, xx])
 
         p_h, p_m, p_l = split3(pan[s, :, h].reshape(PANEL, PANEL))
         small = mul(p_h, i_l, NN) + mul(p_l, i_h, NN) + mul(p_m, i_m, NN)
@@ -454,16 +467,14 @@
     for n in range(NZ):
         wait_bytes(rows.at[0, :, 0], out_sem.at[n])
 
-    for i in range(NX):
-        rows = CHUNK if i == 0 else HALF
+    for i in range(OWN + 1):
         for d in range(1, NZ // 2 + 1):
-            part = chunk(x, z, 0, rows if d < NZ // 2 else rows // 2)
-            wait_bytes(part, up_send.at[i, d])
-            wait_bytes(part, down_send.at[i, d])
+            wait_bytes(piece(i, z, d, 1), up_send.at[i, d])
+            wait_bytes(piece(i, z, d, -1), down_send.at[i, d])
     for j in range(1, NX):
-        wait_bytes(own, x_send.at[j])
-        for d in range(1, NZ):
-            wait_bytes(chunk(x, z, HALF, HALF), side_send.at[d, j])
+        wait_bytes(chunk(x, z, 0, HALF), x_send.at[j])
+        for slot in range(NZ):
+            wait_bytes(chunk(x, z, HALF, HALF), side_send.at[slot, j])
     for kk in range(2):
 
         @pl.when(k == kk)
@@ -479,12 +490,13 @@
             for i in range(1, 4):
                 wait_bytes(cols.at[kk], c_send.at[i])
                 wait_bytes(heads.at[kk], h_send.at[i])
-            for i in range(1, NZ):
-                wait_bytes(turn.at[0, 0:CHUNK, :], sc_send.at[i])
-
-            @pl.when(z != kk)
-            def _():
-                wait_bytes(turn.at[0, 0:CHUNK, :], sc_send.at[0])
+            for part in range(2):
+                for i in range(1, NZ):
+                    wait_bytes(turn.at[0, 0:HALF, :], sc_send.at[part, i])
+
+                @pl.when(z != kk)
+                def _():
+                    wait_bytes(turn.at[0, 0:HALF, :], sc_send.at[part, 0])
 
         @pl.when((r == kk) & in_root_plane)
         def _():
@@ -549,8 +561,8 @@
             pltpu.VMEM((TILE, 512), F32),
             dma((3,)), dma((NZ,)),
             dma((8,)), dma((3,)), dma((16,)), dma, dma((8,)), dma((8,)), dma, dma,
-            dma((8,)), dma((2,)), dma((4,)), dma((4,)),
-            dma((4, 5)), dma((4, 5)), dma((4, 5)), dma((4, 5)), dma((8, 4)), dma((8, 4)),
+            dma((2, 8)), dma((2, 2)), dma((4,)), dma((4,)),
+            dma((5, 5)), dma((5, 5)), dma((5, 5)), dma((5, 5)), dma((8, 4)), dma((8, 4)),
             dma((4,)), dma((2,)), dma((4,)), dma((2,)),
         ],
         compiler_params=pltpu.CompilerParams(collective_id=0, has_side_effects=True, vmem_limit_bytes=46 << 20),

time: 52.5 us -> 49.2 us (0.937)
  the two profiles are of different devices: /device:TPU:16 before, /device:TPU:2 now
where the time goes in v4:
time: 49.2 us; the launch traced here: 49 us
  Pallas kernels  47.7 us (97%)
  local copies, waits for them, and re-layouts  0.69 us (1%)
  between operations  0.65 us (1%)
    pallas_call x1, Pallas kernels, per_device(): pl.pallas_call(gather_kernel, out_shape=[jax.ShapeDtypeStruct((4, NX, 2,...  44.3 us
    pallas_call x1, Pallas kernels, per_device(): pl.pallas_call(update_kernel, out_shape=[jax.ShapeDtypeStruct((2048, 512)...  3.42 us

profile of v4, /device:TPU:2, one launch (start us, length us, event | category | flops | bytes accessed | tf_op | source)
XLA Modules:
  0.0 49.0 jit_solution(18105936115498811204)
XLA Ops:
  0.6 0.0 copy-start
  0.6 0.7 %copy-done = f32[2048]{0:T(1024)S(1)} copy-done((f32[2048]{0:T(1024)S(1)}, f32[2048]{0:T(1024)}, u32[]{:S(2)}) %copy-start) | copy-done | bytes 8216
  1.3 44.3 %shard_map.49 = (f32[4,4,2,64,256]{4,3,2,1,0:T(8,128)S(1)}, f32[2048,512]{1,0:T(8,128)S(1)}, bf16[256,512]{1,0:T(8,128)(2,1)S(1)}, bf16[256,512]{1,0:T(8,128)(2,1)S(1)}, f32[16,128]{1,0:T(8,128)S(1)}) custom-call(f32[2048,512]{1,0:T(8,128)} %cov.1, f32[16,128]{1,0:T(8,128)S(1)} %bitcast.4), custom_call_target="tpu_custom_call" | custom-call | tf_op jit(solution)/shard_map/pallas_call | solution.py:539
  45.6 3.4 %shard_map.50 = (f32[2048,512]{1,0:T(8,128)}, f32[2048,256]{1,0:T(8,128)}, f32[16,128]{1,0:T(8,128)}) custom-call(f32[2048,512]{1,0:T(8,128)S(1)} %get-tuple-element.11.cov, f32[2048,256]{1,0:T(8,128)S(1)} %bitcast.3, bf16[256,512]{1,0:T(8,128)(2,1)S(1)} %get-tuple-element.13.col_high, bf16[256,512]{1,0:T(8,128)(2,1)S(1)} %get-tuple-element.14.col_low, ...), custom_call_target="tpu_custom_call" | custom-call | tf_op jit(solution)/shard_map/pallas_call | solution.py:570
Async XLA Ops:
  0.6 0.7 %copy-start = (f32[2048]{0:T(1024)S(1)}, f32[2048]{0:T(1024)}, u32[]{:S(2)}) copy-start(f32[2048]{0:T(1024)} %param.3) | copy-start | bytes 24580

commit v5 on v4

--- a/solution.py
+++ b/solution.py
@@ -117,10 +117,10 @@
 
 
 def gather_kernel(
-    cov, obs, fac_here, cov_here, col_high, col_low, white,
-    pan, cols, heads, obs_here, rows, inv, acc, lead, turn, work, saved,
-    load_sem, out_sem, l1_send, l1_recv, l2_send, l2_recv, l3_send, l3_recv, sib_send, sib_recv,
-    sc_send, sc_recv, x_send, x_recv, up_send, up_recv, down_send, down_recv, side_send, side_recv,
+    cov, obs, rows, cov_here, col_high, col_low, white,
+    pan, cols, heads, obs_here, inv, acc, lead, turn, work, saved,
+    load_sem, l1_send, l1_recv, l2_send, l2_recv, l3_send, l3_recv, sib_send, sib_recv,
+    sc_send, sc_recv, ring_send, x_recv, up_recv, down_recv, side_recv,
     c_send, c_recv, h_send, h_recv,
 ):
     r, c = lax.axis_index("row"), lax.axis_index("col")
@@ -154,16 +154,17 @@
     def hello(rr, cc):
         pl.semaphore_signal(barrier, inc=1, device_id=dev(rr, cc), device_id_type=MESH)
 
-    for i in range(1, NX):
-        hello(r, x_peer(i))
-    for i in range(1, NZ):
-        hello(r, z_peer(i))
-    for i in range(1, 4):
-        hello((r + 2 * i) % N_ROW, c)
-    hello(sib, c)
     hello(0, x * NZ + r)
     hello(1, x * NZ + r)
     hello(k, z)
+    for i in (4, 3, 5, 2, 6, 1, 7):
+        hello(r, z_peer(i))
+    for i in (2, 1, 3):
+        hello(r, x_peer(i))
+    for i in (2, 1, 3):
+        hello((r + 2 * i) % N_ROW, c)
+    hello(sib, c)
+
     @pl.when(at_source)
     def _():
         pltpu.make_async_copy(cov.at[0:TILE, :], saved, load_sem.at[0]).wait()
@@ -180,7 +181,7 @@
             @pl.when(z != i)
             def _():
                 remote(
-                    cov.at[rows, 0:TILE], lead.at[i, block], l1_send.at[i], l1_recv.at[block], r, i
+                    cov.at[rows, 0:TILE], lead.at[i, block], l1_send, l1_recv.at[block], r, i
                 ).start()
 
             @pl.when(z == i)
@@ -198,6 +199,11 @@
     @pl.when((r == 1) & (c == 1))
     def _():
         level_one(2, 1)
+
+    def kib(n):
+        if n % 16 == 0:
+            return cov_here.at[0 : n // 2, :]
+        return work.at[0:n, :] if n % 8 == 0 else cols.at[0, 0:8, 0 : n * 32]
 
     def wait_bytes(ref, sem):
         pltpu.make_async_copy(ref, ref, sem).wait()
@@ -223,7 +229,7 @@
                         src = turn.at[zz // 2, pl.ds(low, HALF), :]
                         dst = chunk(x, zz, HALF * part, HALF, kk)
                         if i:
-                            remote(src, dst, sc_send.at[part, i], sc_recv.at[kk, part], z, x * NZ + zz).start()
+                            remote(src, dst, sc_send, sc_recv.at[kk, part], z, x * NZ + zz).start()
                         else:
 
                             @pl.when(z == kk)
@@ -232,7 +238,7 @@
 
                             @pl.when(z != kk)
                             def _():
-                                remote(src, dst, sc_send.at[part, i], sc_recv.at[kk, part], z, x * NZ + zz).start()
+                                remote(src, dst, sc_send, sc_recv.at[kk, part], z, x * NZ + zz).start()
 
     for kk in range(2):
 
@@ -247,20 +253,8 @@
                 for xx in (2, 1, 3, 0):
                     if (yy, xx) != (0, 0):
                         remote(
-                            mine(kk), mine(kk), l2_send.at[yy * NX + xx], l2_recv, 2 * yy + kk, xx * NZ + z
+                            mine(kk), mine(kk), l2_send, l2_recv, 2 * yy + kk, xx * NZ + z
                         ).start()
-
-    is_root_line = at_source & in_root_plane
-    for kk in range(2):
-
-        @pl.when(k == kk)
-        def _():
-            @pl.when(jnp.logical_not(is_root_line))
-            def _():
-                wait_bytes(mine(kk), l2_recv)
-
-            for i in (4, 3, 5, 2, 6, 1, 7):
-                remote(mine(kk), mine(kk), l3_send.at[i], l3_recv.at[z], r, z_peer(i)).start()
 
     def stream(i):
         return ((x + i) % NX, 0) if i < OWN else (x, HALF)
@@ -272,9 +266,9 @@
         return chunk(xx, zz, first if way == 1 else first + QUARTER, QUARTER)
 
     def push(i, d, way):
-        send, recv = (up_send, up_recv) if way == 1 else (down_send, down_recv)
+        recv = up_recv if way == 1 else down_recv
         part = piece(i, (z - way * (d - 1) + NZ) % NZ, d, way)
-        remote(part, part, send.at[i, d], recv.at[i, d], r, x * NZ + (z + way + NZ) % NZ).start()
+        remote(part, part, ring_send, recv.at[i, d], r, x * NZ + (z + way + NZ) % NZ).start()
 
     def hop(i, d):
         for way, recv in ((1, up_recv), (-1, down_recv)):
@@ -282,16 +276,16 @@
             if d < NZ // 2:
                 push(i, d + 1, way)
 
-    def sideways(zz, slot):
+    def sideways(zz):
         part = chunk(x, zz, HALF, HALF)
         for j in (2, 1, 3):
-            remote(part, part, side_send.at[slot, j], side_recv.at[zz, x], r, x_peer(j)).start()
+            remote(part, part, ring_send, side_recv.at[zz], r, x_peer(j)).start()
 
     def own_column(d):
         hop(OWN, d)
-        sideways((z - d + NZ) % NZ, d)
+        sideways((z - d + NZ) % NZ)
         if d < NZ // 2:
-            sideways((z + d) % NZ, NZ - d)
+            sideways((z + d) % NZ)
 
     def other_columns(d):
         for i in (1, 3, 2):
@@ -301,14 +295,26 @@
         wait_bytes(chunk(x, z, 0, HALF, kk), sc_recv.at[kk, 0])
     for i in (2, 1, 3):
         part = chunk(x, z, 0, HALF)
-        remote(part, part, x_send.at[i], x_recv.at[x], r, x_peer(i)).start()
+        remote(part, part, ring_send, x_recv.at[x], r, x_peer(i)).start()
     for way in (1, -1):
         push(0, 1, way)
+    is_root_line = at_source & in_root_plane
+    for kk in range(2):
+
+        @pl.when(k == kk)
+        def _():
+            @pl.when(jnp.logical_not(is_root_line))
+            def _():
+                wait_bytes(mine(kk), l2_recv)
+
+            for i in (4, 3, 5, 2, 6, 1, 7):
+                remote(mine(kk), mine(kk), l3_send, l3_recv.at[z], r, z_peer(i)).start()
+
     for kk in range(2):
         wait_bytes(chunk(x, z, HALF, HALF, kk), sc_recv.at[kk, 1])
     for way in (1, -1):
         push(OWN, 1, way)
-    sideways(z, 0)
+    sideways(z)
 
     for kk in range(2):
 
@@ -318,8 +324,8 @@
             pltpu.make_async_copy(obs.at[0:8, :], heads.at[kk], h_recv.at[0]).start()
             for i in range(1, 4):
                 rr = (r + 2 * i) % N_ROW
-                remote(cov.at[0:TILE, :], cols.at[kk], c_send.at[i], c_recv.at[0], rr, c).start()
-                remote(obs.at[0:8, :], heads.at[kk], h_send.at[i], h_recv.at[0], rr, c).start()
+                remote(cov.at[0:TILE, :], cols.at[kk], c_send.at[1], c_recv.at[0], rr, c).start()
+                remote(obs.at[0:8, :], heads.at[kk], h_send.at[1], h_recv.at[0], rr, c).start()
 
     load_cov = pltpu.make_async_copy(cov, cov_here, load_sem.at[1])
     load_cov.start()
@@ -348,17 +354,15 @@
         for way in (1, -1):
             push(i, 1, way)
 
-    for kk in range(2):
-
-        @pl.when(k != kk)
-        def _():
-            wait_bytes(whole(kk), sib_recv)
+    @pl.when(k == 1)
+    def _():
+        wait_bytes(whole(0), sib_recv)
 
     def block(b):
         return lead[:, b].reshape(TILE, TILE)
 
-    FIRST = ((3, lambda: own_column(2)), (4, lambda: hop(0, 2)), (6, lambda: other_columns(1)), )
-    SECOND = ((0, lambda: own_column(3)), (1, lambda: hop(0, 3)), (2, lambda: other_columns(2)), (5, lambda: own_column(4)), (7, lambda: other_columns(3)), )
+    FIRST = ((3, lambda: own_column(2)), (3, lambda: hop(0, 2)), (5, lambda: hop(1, 1)), (6, lambda: hop(3, 1)), (6, lambda: hop(2, 1)), )
+    SECOND = ((0, lambda: own_column(3)), (0, lambda: hop(0, 3)), (1, lambda: hop(1, 2)), (2, lambda: hop(3, 2)), (2, lambda: hop(2, 2)), (5, lambda: own_column(4)), (6, lambda: hop(1, 3)), (7, lambda: hop(3, 3)), (7, lambda: hop(2, 3)), )
     init_work(work, block(0))
 
     def first(g, _):
@@ -375,6 +379,11 @@
     inv_one = triangle(work[:, TILE:], True)
     inv[0:TILE, 0:TILE] = inv_one
     inv[0:TILE, TILE:PANEL] = jnp.zeros((TILE, TILE), F32)
+
+    @pl.when(k == 0)
+    def _():
+        wait_bytes(whole(1), sib_recv)
+
     below = mul6(block(1), inv_one, NT)
     init_work(work, block(2) - mul6(below, below, NT))
     joint = mul6(below, inv_one, NN)
@@ -412,7 +421,6 @@
 
     first_obs = jnp.concatenate([heads[0, 0:1, :], heads[1, 0:1, :]], 1)
     z_row = mul6(jnp.broadcast_to(first_obs, (8, PANEL)), inv[...], NT)[0:1, :]
-    col_high[...], col_low[...] = split2(mul6(inv[...], cols[...].reshape(PANEL, 512), NN))
     i_h, i_m, i_l = split3(inv[...].T)
     lane = lax.broadcasted_iota(jnp.int32, (CHUNK, TILE), 1)
     r_at = lax.broadcasted_iota(jnp.int32, (CHUNK, PANEL), 0)
@@ -423,14 +431,16 @@
         zz = (z + off) % NZ
         s, h = zz // 2, zz % 2
 
+        @pl.when(n == NZ - 2)
+        def _():
+            col_high[...], col_low[...] = split2(mul6(inv[...], cols[...].reshape(PANEL, 512), NN))
+
         @pl.when(n == NZ - 1)
         def _():
             hop(0, NZ // 2)
             other_columns(NZ // 2)
 
-        for i in range(1, NX):
-            xx = (x + i) % NX
-            wait_bytes(chunk(xx, zz, HALF, HALF), side_recv.at[zz, xx])
+        wait_bytes(kib((NX - 1) * HALF), side_recv.at[zz])
 
         p_h, p_m, p_l = split3(pan[s, :, h].reshape(PANEL, PANEL))
         small = mul(p_h, i_l, NN) + mul(p_l, i_h, NN) + mul(p_m, i_m, NN)
@@ -441,7 +451,6 @@
         def _():
             rows[0, 0, h] = jnp.where(c_at <= r_at + CHUNK * h + TILE * r, rows[0, 0, h], 0.0)
 
-        pltpu.make_async_copy(rows.at[s, :, h], fac_here.at[s, :, h], out_sem.at[n]).start()
         here = pl.ds(pl.multiple_of(CHUNK * h, CHUNK), CHUNK)
         sums = acc[here, :]
         for xx in range(NX):
@@ -464,52 +473,38 @@
         white[0:1, :] = z_row[:, TILE:PANEL]
 
     load_cov.wait()
-    for n in range(NZ):
-        wait_bytes(rows.at[0, :, 0], out_sem.at[n])
-
-    for i in range(OWN + 1):
-        for d in range(1, NZ // 2 + 1):
-            wait_bytes(piece(i, z, d, 1), up_send.at[i, d])
-            wait_bytes(piece(i, z, d, -1), down_send.at[i, d])
-    for j in range(1, NX):
-        wait_bytes(chunk(x, z, 0, HALF), x_send.at[j])
-        for slot in range(NZ):
-            wait_bytes(chunk(x, z, HALF, HALF), side_send.at[slot, j])
+
+    passed = 2 * (OWN + 1) * (NZ // 2 - 1) * HALF + 2 * (OWN + 1) * QUARTER
+    wait_bytes(kib(passed + (NX - 1) * (NZ + 1) * HALF), ring_send)
     for kk in range(2):
 
         @pl.when(k == kk)
         def _():
-            for i in range(1, NZ):
-                wait_bytes(mine(kk), l3_send.at[i])
+            wait_bytes(kib((NZ - 1) * (kk + 1) * 8), l3_send)
             wait_bytes(whole(kk), sib_send)
             wait_bytes(cols.at[kk], c_send.at[0])
             wait_bytes(heads.at[kk], h_send.at[0])
 
         @pl.when(r == kk)
         def _():
-            for i in range(1, 4):
-                wait_bytes(cols.at[kk], c_send.at[i])
-                wait_bytes(heads.at[kk], h_send.at[i])
-            for part in range(2):
-                for i in range(1, NZ):
-                    wait_bytes(turn.at[0, 0:HALF, :], sc_send.at[part, i])
-
-                @pl.when(z != kk)
-                def _():
-                    wait_bytes(turn.at[0, 0:HALF, :], sc_send.at[part, 0])
+            wait_bytes(kib(3 * 256), c_send.at[1])
+            wait_bytes(kib(3 * 4), h_send.at[1])
+
+            @pl.when(z != kk)
+            def _():
+                wait_bytes(kib(2 * NZ * 16), sc_send)
+
+            @pl.when(z == kk)
+            def _():
+                wait_bytes(kib(2 * (NZ - 1) * 16), sc_send)
 
         @pl.when((r == kk) & in_root_plane)
         def _():
-            for i in range(1, 16):
-                wait_bytes(mine(kk), l2_send.at[i])
+            wait_bytes(kib(15 * (kk + 1) * 8), l2_send)
 
     @pl.when(((r < 2) & (c == 0)) | ((r == 1) & (c == 1)))
     def _():
-        for i in range(NZ):
-
-            @pl.when(z != i)
-            def _():
-                wait_bytes(lead.at[0, 0], l1_send.at[i])
+        wait_bytes(kib((NZ - 1) * 8), l1_send)
 
 
 def update_kernel(cov, rows, col_high, col_low, white_in, out, fac, white, done, sems):
@@ -546,24 +541,22 @@
             jax.ShapeDtypeStruct((16, TILE), F32),
         ],
         in_specs=[any_space, any_space],
-        out_specs=[any_space, any_space, vmem, vmem, vmem],
+        out_specs=[vmem, any_space, vmem, vmem, vmem],
         scratch_shapes=[
             pltpu.VMEM((4, NX, 2, CHUNK, PANEL), F32),
             pltpu.VMEM((2, TILE, 512), F32),
             pltpu.VMEM((2, 8, TILE), F32),
             pltpu.VMEM((16, TILE), F32),
-            pltpu.VMEM((4, NX, 2, CHUNK, PANEL), F32),
             pltpu.VMEM((PANEL, PANEL), F32),
             pltpu.VMEM((TILE, TILE), F32),
             pltpu.VMEM((NZ, 3, SLICE, TILE), F32),
             pltpu.VMEM((4, TILE, TILE), F32),
             pltpu.VMEM((TILE, PANEL), F32),
             pltpu.VMEM((TILE, 512), F32),
-            dma((3,)), dma((NZ,)),
-            dma((8,)), dma((3,)), dma((16,)), dma, dma((8,)), dma((8,)), dma, dma,
-            dma((2, 8)), dma((2, 2)), dma((4,)), dma((4,)),
-            dma((5, 5)), dma((5, 5)), dma((5, 5)), dma((5, 5)), dma((8, 4)), dma((8, 4)),
-            dma((4,)), dma((2,)), dma((4,)), dma((2,)),
+            dma((3,)),
+            dma, dma((3,)), dma, dma, dma, dma((8,)), dma, dma,
+            dma, dma((2, 2)), dma, dma((4,)), dma((5, 5)), dma((5, 5)), dma((8,)),
+            dma((2,)), dma((2,)), dma((2,)), dma((2,)),
         ],
         compiler_params=pltpu.CompilerParams(collective_id=0, has_side_effects=True, vmem_limit_bytes=46 << 20),
     )(covariance, obs)

time: 49.2 us -> 46.5 us (0.945)
  the two profiles are of different devices: /device:TPU:2 before, /device:TPU:16 now
where the time goes in v5:
time: 46.5 us; the launch traced here: 45.7 us
  Pallas kernels  44.3 us (95%)
  local copies, waits for them, and re-layouts  0.69 us (1%)
  between operations  0.65 us (1%)
    pallas_call x1, Pallas kernels, per_device(): pl.pallas_call(gather_kernel, out_shape=[jax.ShapeDtypeStruct((4, NX, 2,...  40.9 us
    pallas_call x1, Pallas kernels, per_device(): pl.pallas_call(update_kernel, out_shape=[jax.ShapeDtypeStruct((2048, 512)...  3.41 us

profile of v5, /device:TPU:16, one launch (start us, length us, event | category | flops | bytes accessed | tf_op | source)
XLA Modules:
  0.0 45.7 jit_solution(12812905951204012893)
XLA Ops:
  0.6 0.0 copy-start
  0.6 0.7 %copy-done = f32[2048]{0:T(1024)S(1)} copy-done((f32[2048]{0:T(1024)S(1)}, f32[2048]{0:T(1024)}, u32[]{:S(2)}) %copy-start) | copy-done | bytes 8216
  1.3 40.9 %shard_map.49 = (f32[4,4,2,64,256]{4,3,2,1,0:T(8,128)S(1)}, f32[2048,512]{1,0:T(8,128)S(1)}, bf16[256,512]{1,0:T(8,128)(2,1)S(1)}, bf16[256,512]{1,0:T(8,128)(2,1)S(1)}, f32[16,128]{1,0:T(8,128)S(1)}) custom-call(f32[2048,512]{1,0:T(8,128)} %cov.1, f32[16,128]{1,0:T(8,128)S(1)} %bitcast.4), custom_call_target="tpu_custom_call" | custom-call | tf_op jit(solution)/shard_map/pallas_call | solution.py:534
  42.3 3.4 %shard_map.50 = (f32[2048,512]{1,0:T(8,128)}, f32[2048,256]{1,0:T(8,128)}, f32[16,128]{1,0:T(8,128)}) custom-call(f32[2048,512]{1,0:T(8,128)S(1)} %get-tuple-element.11.cov, f32[2048,256]{1,0:T(8,128)S(1)} %bitcast.3, bf16[256,512]{1,0:T(8,128)(2,1)S(1)} %get-tuple-element.13.col_high, bf16[256,512]{1,0:T(8,128)(2,1)S(1)} %get-tuple-element.14.col_low, ...), custom_call_target="tpu_custom_call" | custom-call | tf_op jit(solution)/shard_map/pallas_call | solution.py:563
Async XLA Ops:
  0.6 0.7 %copy-start = (f32[2048]{0:T(1024)S(1)}, f32[2048]{0:T(1024)}, u32[]{:S(2)}) copy-start(f32[2048]{0:T(1024)} %param.3) | copy-start | bytes 24580
